TPU v7x, 512 devices: a whole 4x4x16 slice. The times are simulated.
512 devices in a mesh: row: 16 (over z_hi, x, core), col: 4 (over y), depth: 8 (over z_lo).
Axes of the slice: x: 4, y: 4, z: 16 (z_hi: 2, z_lo: 8; z = z_hi * 8 + z_lo), core: 2. Of those that a mesh axis runs over, the one named last changes fastest.
Arguments:
- activations: bfloat16 [16384, 4544], P(('depth', 'row'), 'col'), may hold values from -6 to 6
- out_grads: bfloat16 [16384, 12288], P(('depth', 'col'), 'row'), may hold values from -0.09375 to 0.09375
Outputs:
- weight_grad: float32 [12288, 4544], P(('row', 'depth'), 'col')
All inputs are finite; a program needn't handle non-finite values.
Results may differ from a plain program's by a relative error of at most 0.0003.
Values may be sent and summed in bfloat16 or wider, within the bound.
No kernel may reach another device: no remote copies, remote signals or barrier semaphores. Data moves between devices by JAX's collectives and lax.ppermute only.
A program may use at most 64 MiB of HBM per device.

v0:
```python
import jax
import jax.numpy as jnp
from jax import lax
from jax.sharding import PartitionSpec as P


def contract(left, right):
    return lax.dot_general(
        left, right, (((0,), (0,)), ((), ())), preferred_element_type=jnp.float32
    )


def gather_acts(activations):
    return lax.all_gather(activations, "row", axis=0, tiled=True)


def body(activations, out_grads):
    whole_acts = gather_acts(activations)
    partial_tile = contract(lax.all_gather(out_grads, "col", axis=0, tiled=True), whole_acts)
    return lax.psum_scatter(partial_tile, "depth", scatter_dimension=0, tiled=True)


def solution(mesh):
    in_specs = (P(("depth", "row"), "col"), P(("depth", "col"), "row"))
    out_specs = P(("row", "depth"), "col")
    return jax.shard_map(body, mesh=mesh, in_specs=in_specs, out_specs=out_specs, check_vma=False)
```

profile of v0, /device:TPU:1, one launch (start us, length us, event | category | flops | bytes accessed | tf_op | source)
XLA Modules:
  0.0 293.2 jit_solution(5465479792485687859)
XLA Ops:
  6.5 0.0 all-gather.3.cloned.1.call-start
  6.5 0.7 all-gather.3.cloned.1.call-update
  7.3 0.0 all-gather.5.cloned.1.call-start
  7.3 0.7 all-gather.5.cloned.1.call-update
  8.0 0.0 reduce-scatter.2.cloned.1.call-start
  8.1 54.0 %all-gather.3.cloned.1.call-done = bf16[2048,768]{1,0:T(8,128)(2,1)} async-done(((bf16[512,768]{1,0:T(8,128)(2,1)}), bf16[2048,768]{1,0:T(8,128)(2,1)}) %all-gather.3.cloned.1.call-update) | async-done | bytes 3145744 | tf_op jit(solution)/shard_map/all_gather | solution.py:19
  62.0 132.4 %all-gather.5.cloned.1.call-done = bf16[2048,1136]{0,1:T(8,128)(2,1)} async-done(((bf16[128,1136]{0,1:T(8,128)(2,1)}), bf16[2048,1136]{0,1:T(8,128)(2,1)}) %all-gather.5.cloned.1.call-update) | async-done | bytes 4653072 | tf_op jit(solution)/shard_map/all_gather | solution.py:14
  194.4 9.3 %fusion = f32[768,1136]{1,0:T(8,128)} fusion(bf16[2048,768]{1,0:T(8,128)(2,1)} %all-gather.3.cloned.1.call-done, bf16[2048,1136]{0,1:T(8,128)(2,1)} %all-gather.5.cloned.1.call-done), kind=kOutput, calls=%fused_computation | convolution fusion | flops 3573547008 | bytes 11288576 | tf_op jit(solution)/shard_map/dot_general | solution.py:8
  203.7 0.0 reduce-scatter.2.cloned.1.call-update
  203.8 82.9 %reduce-scatter.2.cloned.1.call-done = f32[96,1136]{1,0:T(8,128)} async-done(((f32[768,1136]{1,0:T(8,128)}), f32[96,1136]{1,0:T(8,128)}) %reduce-scatter.2.cloned.1.call-update) | async-done | bytes 436240 | tf_op jit(solution)/shard_map/reduce_scatter | solution.py:20
Async XLA Ops:
  6.5 55.5 %all-gather.3.cloned.1.call-start = ((), (), s32[]{:S(2)}) async-start(), calls=%async_computation.1 | async-start | bytes 3932160 | tf_op jit(solution)/shard_map/all_gather | solution.py:19
  7.3 187.2 %all-gather.5.cloned.1.call-start = ((), (), s32[]{:S(2)}) async-start(), calls=%async_computation.2 | async-start | bytes 4943872 | tf_op jit(solution)/shard_map/all_gather | solution.py:14
  8.0 278.6 %reduce-scatter.2.cloned.1.call-start = ((), (), s32[]{:S(2)}) async-start(), calls=%async_computation.3 | async-start | bytes 3981312 | tf_op jit(solution)/shard_map/reduce_scatter | solution.py:20
Sparse Core Ops, SparseCore 0:
  9.5 52.5 all-gather.2
  65.2 129.2 all-gather.4
  203.9 82.7 reduce-scatter.1
where the time goes:
time: 293 us
  waiting for transfers between devices  271 us (92%)
  between operations  13.1 us (4%)
  matrix products  9.3 us (3%)
    all_gather x1, waiting for transfers between devices, gather_acts(): return lax.all_gather(activations, 'row', axis=0, tiled=True)  132 us
    reduce_scatter x1, waiting for transfers between devices, body(): lax.psum_scatter(partial_tile, 'depth', scatter_dimension=0, tiled=True)  82.9 us
    all_gather x1, waiting for transfers between devices, body(): lax.all_gather(out_grads, 'col', axis=0, tiled=True)  54 us
    dot_general x1, matrix products, contract(): lax.dot_general(left, right, (((0,), (0,)), ((), ())), preferred_element_...  9.3 us
  transfers between devices with their start and end apart: 3, of which 3 were waited for; matrix products, arithmetic and copies ran while one was open for 0% of the time, Pallas kernels for 0%

commit v1 on v0

v1 whole, which is shorter than its diff:
```python
import functools
import jax
import jax.numpy as jnp
from jax import lax
from jax.experimental import pallas as pl
from jax.experimental.pallas import tpu as pltpu
from jax.sharding import PartitionSpec as P

AXES = ("row", "col", "depth")
SIZES = (2, 4, 2, 4, 8)


def permute(value, target):
    pairs = []
    for zh in range(2):
        for x in range(4):
            for core in range(2):
                for y in range(4):
                    for zl in range(8):
                        to = target(zh, x, core, y, zl)
                        if to is not None:
                            flat = lambda c: ((((c[0] * 4 + c[1]) * 2 + c[2]) * 4 + c[3]) * 8 + c[4])
                            pairs.append((flat((zh, x, core, y, zl)), flat(to)))
    return lax.ppermute(value, AXES, pairs)


def over_x(value, step):
    return permute(value, lambda zh, x, c, y, zl: (zh, (x - step) % 4, c, y, zl))


def over_y(value, step):
    return permute(value, lambda zh, x, c, y, zl: (zh, x, c, (y - step) % 4, zl))


def other_core(value):
    return permute(value, lambda zh, x, c, y, zl: (zh, x, 1 - c, y, zl))


def other_half(value):
    return permute(value, lambda zh, x, c, y, zl: (1 - zh, x, c, y, zl))


def other_quad(value):
    return permute(value, lambda zh, x, c, y, zl: (zh, x, c, y, zl ^ 4))


def depth_pair(value, bit):
    return permute(value, lambda zh, x, c, y, zl: (zh, x, c, y, zl ^ bit))


NT = (((1,), (1,)), ((), ()))
TILES = ((0, 256), (256, 512), (512, 768), (768, 1024), (1024, 1136))
f16, f32, bf16 = jnp.float16, jnp.float32, jnp.bfloat16
PARAMS = pltpu.CompilerParams(vmem_limit_bytes=40 * 2**20)
VM = pl.BlockSpec(memory_space=pltpu.VMEM)
SM = pl.BlockSpec(memory_space=pltpu.SMEM)
ANY = pl.BlockSpec(memory_space=pl.ANY)


def cost(us):
    return pl.CostEstimate(flops=int(us * 1e9), bytes_accessed=2**20, transcendentals=0)


def shape(dims, dtype):
    return jax.ShapeDtypeStruct(dims, dtype)


def tie(*values):
    return lax.optimization_barrier(values)


def lanes_at(start, size):
    return pl.ds(pl.multiple_of(start, 128), size)


def fence_kernel(ref, out_ref):
    out_ref[...] = ref[...]


def prep_kernel(at_ref, all_ref, grads_ref, fetched, turned, sems):
    zh, zl = at_ref[0], at_ref[4]
    b0, b1, quad = lax.rem(zl, 2), lax.rem(zl // 2, 2), zl // 4
    copies = [pltpu.make_async_copy(all_ref.at[pl.ds(j * 512, 512), :], fetched.at[j], sems.at[j]) for j in range(4)]
    for copy in copies:
        copy.start()
    for j, copy in enumerate(copies):
        copy.wait()
        turned[...] = fetched[j].T
        slot = lax.rem(j - 2 * zh + 4, 4)
        for k in range(8):
            owner_quad = 1 - quad if k < 4 else quad
            owner_b0 = 1 - b0 if k % 4 < 2 else b0
            owner_b1 = 1 - b1 if k % 2 == 0 else b1
            first = (owner_quad * 4 + owner_b1 * 2 + owner_b0) * 96
            grads_ref[slot, k * 96:(k + 1) * 96, :] = turned[pl.ds(pl.multiple_of(first, 32), 96), :]


def spread(at_ref, own, other, acts_ref, sems):
    x, core = at_ref[1], at_ref[2]
    copies = []
    for xr in range(4):
        slot = lax.rem(x + xr, 4) * 256
        for i, (src, c) in enumerate(((own, core), (other, 1 - core))):
            copies.append(pltpu.make_async_copy(src.at[xr], acts_ref.at[:, lanes_at(slot + c * 128, 128)], sems.at[2 * xr + i]))
    for copy in copies:
        copy.start()
    return copies


def own_kernel(at_ref, s0, t0, grads_ref, token, out_ref, acts_ref, sems):
    for copy in spread(at_ref, s0, t0, acts_ref, sems):
        copy.wait()
    for lo, hi in TILES:
        out_ref[:, lo:hi] = sum(
            lax.dot_general(grads_ref[j], acts_ref[lo:hi, j * 512:(j + 1) * 512], NT, preferred_element_type=f32) for j in range(2))


def rest_kernel(at_ref, s1, t1, grads_ref, start_ref, far_ref, near_ref, keep_far_ref, keep_near_ref, acts_ref, sems):
    for copy in spread(at_ref, s1, t1, acts_ref, sems):
        copy.wait()
    top = None
    for lo, hi in TILES:
        part = start_ref[:, lo:hi] + sum(
            lax.dot_general(grads_ref[2 + j], acts_ref[lo:hi, j * 512:(j + 1) * 512], NT, preferred_element_type=f32) for j in range(2))
        far_ref[:, lo:hi] = part[:192]
        keep_far_ref[:, lo:hi] = part[192:384]
        near_ref[:, lo:hi] = part[384:576]
        keep_near_ref[:, lo:hi] = part[576:]
        part = jnp.max(jnp.abs(part), axis=0, keepdims=True)
        part = jnp.max(part, axis=1, keepdims=True)
        top = part if top is None else jnp.maximum(top, part)
    size = jnp.clip(jnp.ceil(jnp.log2(top)) + 1, -100, 100)
    scale = jnp.exp2(15 - size)
    for ref in (far_ref, near_ref):
        ref[:, :1136] = ref[:, :1136] * scale
    for ref in (far_ref, near_ref, keep_far_ref, keep_near_ref):
        ref[:, 1136:] = jnp.broadcast_to(size, (192, 16))


def add(keep, message):
    message = message.astype(f32)
    size = message[:, 1136:1137]
    total = keep + message * jnp.exp2(size - 15)
    return total, jnp.maximum(keep[:, 1136:1137], size) + 1


def tagged(total, size, scale):
    return jnp.where(lax.broadcasted_iota(jnp.int32, total.shape, 1) < 1136, total * scale, size)


def wrap(total, size):
    return tagged(total, size, jnp.exp2(15 - size)).astype(f16)


def again(token):
    return pl.pallas_call(
        fence_kernel, out_shape=shape((8, 128), f32), in_specs=[VM], out_specs=VM, compiler_params=PARAMS, name="fence",
    )(token)


def body(activations, out_grads):
    row, y, zl = (lax.axis_index(a) for a in AXES)
    where = jnp.stack([row // 8, row // 2 % 4, row % 2, y, zl]).astype(jnp.int32)
    bt = activations.T
    token = again(jnp.zeros((8, 128), f32) + row.astype(f32))
    every_grad = lax.all_gather(out_grads, "col", axis=0, tiled=True)
    bt, token = tie(bt, token)
    swapped = other_half(bt)
    x1, x2, x3 = (over_x(bt, s) for s in (1, 2, 3))
    swapped, token = tie(swapped, token)
    token = again(token)
    x1, x2, x3, swapped, token = tie(x1, x2, x3, swapped, token)
    s0 = jnp.stack([bt, x1, x2, x3])
    t0 = other_core(s0)
    o1, o2, o3 = (over_x(swapped, s) for s in (1, 2, 3))
    grads = pl.pallas_call(
        prep_kernel, out_shape=shape((4, 768, 512), bf16),
        in_specs=[SM, ANY], out_specs=VM, compiler_params=PARAMS, name="prep",
        scratch_shapes=[pltpu.VMEM((4, 512, 768), bf16), pltpu.VMEM((768, 512), bf16), pltpu.SemaphoreType.DMA((4,))],
    )(where, every_grad)
    o1, o2, o3, grads = tie(o1, o2, o3, grads)
    s1 = jnp.stack([swapped, o1, o2, o3])
    t1 = other_core(s1)
    t0, s1 = tie(t0, s1)
    start = pl.pallas_call(
        own_kernel, out_shape=shape((768, 1136), f32),
        in_specs=[SM] + [ANY] * 2 + [VM] * 2, out_specs=VM, compiler_params=PARAMS, name="own",
        scratch_shapes=[pltpu.VMEM((1136, 1024), bf16), pltpu.SemaphoreType.DMA((8,))],
    )(where, s0, t0, grads, token)
    t1, start = tie(t1, start)
    far, near, keep_far, keep_near = pl.pallas_call(
        rest_kernel, out_shape=(shape((192, 1152), f32),) * 4,
        in_specs=[SM] + [ANY] * 2 + [VM] * 2, out_specs=(VM,) * 4, compiler_params=PARAMS, name="rest",
        scratch_shapes=[pltpu.VMEM((1136, 1024), bf16), pltpu.SemaphoreType.DMA((8,))],
    )(where, s1, t1, grads, start)
    f1, n1 = depth_pair(far.astype(f16), 1), depth_pair(near.astype(f16), 1)
    far, size = add(keep_far, f1)
    f2 = depth_pair(wrap(far[:96], size[:96]), 2)
    n1, far = tie(n1, tagged(far[96:], size[96:], 1))
    near, size = add(keep_near, n1)
    n2 = depth_pair(wrap(near[:96], size[:96]), 2)
    crossed = depth_pair(wrap(*add(far, f2)), 4)
    near, size = add(tagged(near[96:], size[96:], 1), n2)
    near, crossed = tie(tagged(near, size, 1), crossed)
    return add(near, crossed)[0][:, :1136]


def solution(mesh):
    in_specs = (P(("depth", "row"), "col"), P(("depth", "col"), "row"))
    out_specs = P(("row", "depth"), "col")
    return jax.shard_map(body, mesh=mesh, in_specs=in_specs, out_specs=out_specs, check_vma=False)
```

time: 293 us -> 149 us (0.51)
  waiting for transfers between devices: 271 us -> 63.1 us
  starting transfers between devices: 0.08 us -> 55.7 us
  Pallas kernels: 0 us -> 9.41 us
  matrix products: 9.3 us -> 0 us
  other arithmetic: 0 us -> 4.68 us
    all_gather x2 -> x1, waiting for transfers between devices: 186 us -> 3.79 us  [body(): every_grad = lax.all_gather(out_grads, 'col', axis=0, tiled=True)]
    reduce_scatter x1 -> x0, waiting for transfers between devices: 82.9 us -> none  [body(): lax.psum_scatter(partial_tile, 'depth', scatter_dimension=0, tiled=True)]
    ppermute x0 -> x14, waiting for transfers between devices: none -> 58.6 us  [permute(): return lax.ppermute(value, AXES, pairs)]
    ppermute x0 -> x14, starting transfers between devices: none -> 55.7 us  [permute(): return lax.ppermute(value, AXES, pairs)]
    pallas_call x0 -> x5, Pallas kernels: none -> 9.41 us  [the longest x1 3.81 us: body(): pl.pallas_call(rest_kernel, out_shape=(shape((192, 1152), f32),) * 4, in_...]
    dot_general x1 -> x0, matrix products: 9.3 us -> none  [contract(): lax.dot_general(left, right, (((0,), (0,)), ((), ())), preferred_element_...]
  transfers between devices with their start and end apart: 3 -> 15, of which waited for: 3 -> 10; matrix products, arithmetic and copies ran while one was open for 0% -> 2% of each run, Pallas kernels for 0% -> 4%
where the time goes in v1:
time: 149 us
  waiting for transfers between devices  63.1 us (42%)
  starting transfers between devices  55.7 us (37%)
  between operations  13.7 us (9%)
  Pallas kernels  9.41 us (6%)
  other arithmetic  4.68 us (3%)
  local copies, waits for them, and re-layouts  1.98 us (1%)
    ppermute x14, waiting for transfers between devices, permute(): return lax.ppermute(value, AXES, pairs)  58.6 us
    ppermute x14, starting transfers between devices, permute(): return lax.ppermute(value, AXES, pairs)  55.7 us
    pallas_call x1, Pallas kernels, body(): pl.pallas_call(rest_kernel, out_shape=(shape((192, 1152), f32),) * 4, in_...  3.81 us
    all_gather x1, waiting for transfers between devices, body(): every_grad = lax.all_gather(out_grads, 'col', axis=0, tiled=True)  3.79 us
    pallas_call x1, Pallas kernels, body(): pl.pallas_call(own_kernel, out_shape=shape((768, 1136), f32), in_specs=[S...  3.56 us
  transfers between devices with their start and end apart: 15, of which 10 were waited for; matrix products, arithmetic and copies ran while one was open for 2% of the time, Pallas kernels for 4%

profile of v1, /device:TPU:1, one launch (start us, length us, event | category | flops | bytes accessed | tf_op | source)
XLA Modules:
  0.0 148.6 jit_solution(1737982407173041668)
XLA Ops:
  7.3 16.3 %collective-permute-start.3 = (bf16[1136,128]{1,0:T(8,128)(2,1)}, bf16[1136,128]{1,0:T(8,128)(2,1)S(1)}, u32[]{:S(2)}, u32[]{:S(2)}) collective-permute-start(bf16[1136,128]{1,0:T(8,128)(2,1)} %bitcast.14), channel_id=1, source_target_pairs={{0,256},{1,257},{2,258},{3,259},{4,260},{5,261},{6,262},{7,263},{8... | collective-permute-start | bytes 872456 | tf_op jit(solution)/shard_map/ppermute | solution.py:24
  23.6 4.4 %collective-permute-start = (bf16[1136,128]{1,0:T(8,128)(2,1)}, bf16[1136,128]{1,0:T(8,128)(2,1)S(1)}, u32[]{:S(2)}, u32[]{:S(2)}) collective-permute-start(bf16[1136,128]{1,0:T(8,128)(2,1)} %bitcast.15), channel_id=1, source_target_pairs={{0,192},{1,193},{2,194},{3,195},{4,196},{5,197},{6,198},{7,199},{8... | collective-permute-start | bytes 872456 | tf_op jit(solution)/shard_map/ppermute | solution.py:24
  28.0 2.4 %collective-permute-start.1 = (bf16[1136,128]{1,0:T(8,128)(2,1)}, bf16[1136,128]{1,0:T(8,128)(2,1)S(1)}, u32[]{:S(2)}, u32[]{:S(2)}) collective-permute-start(bf16[1136,128]{1,0:T(8,128)(2,1)} %bitcast.16), channel_id=1, source_target_pairs={{0,128},{1,129},{2,130},{3,131},{4,132},{5,133},{6,134},{7,135},{8... | collective-permute-start | bytes 872456 | tf_op jit(solution)/shard_map/ppermute | solution.py:24
  30.4 2.5 %collective-permute-start.2 = (bf16[1136,128]{1,0:T(8,128)(2,1)}, bf16[1136,128]{1,0:T(8,128)(2,1)S(1)}, u32[]{:S(2)}, u32[]{:S(2)}) collective-permute-start(bf16[1136,128]{1,0:T(8,128)(2,1)} %bitcast.17), channel_id=1, source_target_pairs={{0,64},{1,65},{2,66},{3,67},{4,68},{5,69},{6,70},{7,71},{8,72},{9,... | collective-permute-start | bytes 872456 | tf_op jit(solution)/shard_map/ppermute | solution.py:24
  34.3 4.5 %collective-permute-done.1 = bf16[1136,128]{1,0:T(8,128)(2,1)S(1)} collective-permute-done((bf16[1136,128]{1,0:T(8,128)(2,1)}, bf16[1136,128]{1,0:T(8,128)(2,1)S(1)}, u32[]{:S(2)}, u32[]{:S(2)}) %collective-permute-start.1) | collective-permute-done | bytes 290848 | tf_op jit(solution)/shard_map/ppermute | solution.py:24
  38.8 8.0 %collective-permute-done.2 = bf16[1136,128]{1,0:T(8,128)(2,1)S(1)} collective-permute-done((bf16[1136,128]{1,0:T(8,128)(2,1)}, bf16[1136,128]{1,0:T(8,128)(2,1)S(1)}, u32[]{:S(2)}, u32[]{:S(2)}) %collective-permute-start.2) | collective-permute-done | bytes 290848 | tf_op jit(solution)/shard_map/ppermute | solution.py:24
  48.7 2.3 %collective-permute-start.6 = (bf16[1136,128]{1,0:T(8,128)(2,1)S(1)}, bf16[1136,128]{1,0:T(8,128)(2,1)S(1)}, u32[]{:S(2)}, u32[]{:S(2)}) collective-permute-start(bf16[1136,128]{1,0:T(8,128)(2,1)S(1)} %collective-permute-done.3), channel_id=1, source_target_pairs={{0,128},{1,129},{2,130},{3,131},{4,132},{5,133},{6,134},{7,135},{8... | collective-permute-start | bytes 872456 | tf_op jit(solution)/shard_map/ppermute | solution.py:24
  51.0 2.9 %collective-permute-start.7 = (bf16[1136,128]{1,0:T(8,128)(2,1)S(1)}, bf16[1136,128]{1,0:T(8,128)(2,1)S(1)}, u32[]{:S(2)}, u32[]{:S(2)}) collective-permute-start(bf16[1136,128]{1,0:T(8,128)(2,1)S(1)} %collective-permute-done.3), channel_id=1, source_target_pairs={{0,64},{1,65},{2,66},{3,67},{4,68},{5,69},{6,70},{7,71},{8,72},{9,... | collective-permute-start | bytes 872456 | tf_op jit(solution)/shard_map/ppermute | solution.py:24
  55.2 3.0 %collective-permute-start.4 = (bf16[4,1136,128]{2,1,0:T(8,128)(2,1)S(1)}, bf16[4,1136,128]{2,1,0:T(8,128)(2,1)S(1)}, u32[]{:S(2)}, u32[]{:S(2)}) collective-permute-start(bf16[4,1136,128]{2,1,0:T(8,128)(2,1)S(1)} %pad_maximum_fusion.s0), channel_id=1, source_target_pairs={{0,32},{1,33},{2,34},{3,35},{4,36},{5,37},{6,38},{7,39},{8,40},{9,... | collective-permute-start | bytes 3489800 | tf_op jit(solution)/shard_map/ppermute | solution.py:24
  58.3 3.8 %all-gather.2.cloned.1.call-done.all_ref = bf16[2048,768]{1,0:T(8,128)(2,1)} async-done(((bf16[512,768]{1,0:T(8,128)(2,1)}), bf16[2048,768]{1,0:T(8,128)(2,1)}) %all-gather.2.cloned.1.call-update) | async-done | bytes 3145744 | tf_op jit(solution)/shard_map/all_gather | solution.py:166
  63.9 2.0 %prep.1.grads_ref = bf16[4,768,512]{2,1,0:T(8,128)(2,1)S(1)} custom-call(s32[5]{0:T(128)S(1)} %stack.53.at_ref, bf16[2048,768]{1,0:T(8,128)(2,1)S(1)} %copy-done), custom_call_target="tpu_custom_call" | custom-call | tf_op jit(solution)/shard_map/prep/pallas_call | solution.py:176
  67.3 2.4 %collective-permute-start.8 = (bf16[4,1136,128]{2,1,0:T(8,128)(2,1)S(1)}, bf16[4,1136,128]{2,1,0:T(8,128)(2,1)S(1)}, u32[]{:S(2)}, u32[]{:S(2)}) collective-permute-start(bf16[4,1136,128]{2,1,0:T(8,128)(2,1)S(1)} %pad_maximum_fusion.1.s1), channel_id=1, source_target_pairs={{0,32},{1,33},{2,34},{3,35},{4,36},{5,37},{6,38},{7,39},{8,40},{9,... | collective-permute-start | bytes 3489800 | tf_op jit(solution)/shard_map/ppermute | solution.py:24
  69.7 3.6 %own.1.start_ref = f32[768,1136]{1,0:T(8,128)S(1)} custom-call(s32[5]{0:T(128)S(1)} %stack.53.at_ref, bf16[4,1136,128]{2,1,0:T(8,128)(2,1)S(1)} %pad_maximum_fusion.s0, bf16[4,1136,128]{2,1,0:T(8,128)(2,1)S(1)} %collective-permute-done.4.t0, bf16[4,768,512]{2,1,0:T(8,128)(2,1)S(1)} %prep.1.grads_ref, f32[8,128]{1,0:T(8,128)S(1)} %fence.3.token), custom_call_target="tpu_custom_call" | custom-call | tf_op jit(solution)/shard_map/own/pallas_call | solution.py:185
  73.3 3.8 %rest.1 = (f32[192,1152]{1,0:T(8,128)S(1)}, f32[192,1152]{1,0:T(8,128)S(1)}, f32[192,1152]{1,0:T(8,128)S(1)}, f32[192,1152]{1,0:T(8,128)S(1)}) custom-call(s32[5]{0:T(128)S(1)} %stack.53.at_ref, bf16[4,1136,128]{2,1,0:T(8,128)(2,1)S(1)} %pad_maximum_fusion.1.s1, bf16[4,1136,128]{2,1,0:T(8,128)(2,1)S(1)} %collective-permute-done.8.t1, ...), custom_call_target="tpu_custom_call" | custom-call | tf_op jit(solution)/shard_map/rest/pallas_call | solution.py:191
  77.2 7.0 %collective-permute-start.10 = (f16[192,1152]{1,0:T(8,128)(2,1)S(1)}, f16[192,1152]{1,0:T(8,128)(2,1)S(1)}, u32[]{:S(2)}, u32[]{:S(2)}) collective-permute-start(f16[192,1152]{1,0:T(8,128)(2,1)S(1)} %convert_element_type.35), channel_id=1, source_target_pairs={{0,1},{1,0},{2,3},{3,2},{4,5},{5,4},{6,7},{7,6},{8,9},{9,8},{10,11... | collective-permute-start | bytes 1327112 | tf_op jit(solution)/shard_map/ppermute | solution.py:24
  84.3 1.9 %collective-permute-start.9 = (f16[192,1152]{1,0:T(8,128)(2,1)S(1)}, f16[192,1152]{1,0:T(8,128)(2,1)S(1)}, u32[]{:S(2)}, u32[]{:S(2)}) collective-permute-start(f16[192,1152]{1,0:T(8,128)(2,1)S(1)} %convert_element_type.34), channel_id=1, source_target_pairs={{0,1},{1,0},{2,3},{3,2},{4,5},{5,4},{6,7},{7,6},{8,9},{9,8},{10,11... | collective-permute-start | bytes 1327112 | tf_op jit(solution)/shard_map/ppermute | solution.py:24
  86.2 8.5 %collective-permute-done.10 = f16[192,1152]{1,0:T(8,128)(2,1)S(1)} collective-permute-done((f16[192,1152]{1,0:T(8,128)(2,1)S(1)}, f16[192,1152]{1,0:T(8,128)(2,1)S(1)}, u32[]{:S(2)}, u32[]{:S(2)}) %collective-permute-start.10) | collective-permute-done | bytes 442400 | tf_op jit(solution)/shard_map/ppermute | solution.py:24
  95.5 1.9 %collective-permute-start.12 = (f16[96,1152]{1,0:T(8,128)(2,1)S(1)}, f16[96,1152]{1,0:T(8,128)(2,1)S(1)}, u32[]{:S(2)}, u32[]{:S(2)}) collective-permute-start(f16[96,1152]{1,0:T(8,128)(2,1)S(1)} %get-tuple-element.66), channel_id=1, source_target_pairs={{0,2},{1,3},{2,0},{3,1},{4,6},{5,7},{6,4},{7,5},{8,10},{9,11},{10,... | collective-permute-start | bytes 663560 | tf_op jit(solution)/shard_map/ppermute | solution.py:24
  97.4 7.8 %collective-permute-done.9 = f16[192,1152]{1,0:T(8,128)(2,1)S(1)} collective-permute-done((f16[192,1152]{1,0:T(8,128)(2,1)S(1)}, f16[192,1152]{1,0:T(8,128)(2,1)S(1)}, u32[]{:S(2)}, u32[]{:S(2)}) %collective-permute-start.9) | collective-permute-done | bytes 442400 | tf_op jit(solution)/shard_map/ppermute | solution.py:24
  105.8 3.5 %collective-permute-done.12 = f16[96,1152]{1,0:T(8,128)(2,1)S(1)} collective-permute-done((f16[96,1152]{1,0:T(8,128)(2,1)S(1)}, f16[96,1152]{1,0:T(8,128)(2,1)S(1)}, u32[]{:S(2)}, u32[]{:S(2)}) %collective-permute-start.12) | collective-permute-done | bytes 221216 | tf_op jit(solution)/shard_map/ppermute | solution.py:24
  109.9 3.6 %collective-permute-start.11 = (f16[96,1152]{1,0:T(8,128)(2,1)S(1)}, f16[96,1152]{1,0:T(8,128)(2,1)S(1)}, u32[]{:S(2)}, u32[]{:S(2)}) collective-permute-start(f16[96,1152]{1,0:T(8,128)(2,1)S(1)} %get-tuple-element.68), channel_id=1, source_target_pairs={{0,2},{1,3},{2,0},{3,1},{4,6},{5,7},{6,4},{7,5},{8,10},{9,11},{10,... | collective-permute-start | bytes 663560 | tf_op jit(solution)/shard_map/ppermute | solution.py:24
  113.5 3.0 %collective-permute-start.13 = (f16[96,1152]{1,0:T(8,128)(2,1)S(1)}, f16[96,1152]{1,0:T(8,128)(2,1)S(1)}, u32[]{:S(2)}, u32[]{:S(2)}) collective-permute-start(f16[96,1152]{1,0:T(8,128)(2,1)S(1)} %get-tuple-element.74), channel_id=1, source_target_pairs={{0,4},{1,5},{2,6},{3,7},{4,0},{5,1},{6,2},{7,3},{8,12},{9,13},{10,... | collective-permute-start | bytes 663560 | tf_op jit(solution)/shard_map/ppermute | solution.py:24
  116.5 3.9 %collective-permute-done.11 = f16[96,1152]{1,0:T(8,128)(2,1)S(1)} collective-permute-done((f16[96,1152]{1,0:T(8,128)(2,1)S(1)}, f16[96,1152]{1,0:T(8,128)(2,1)S(1)}, u32[]{:S(2)}, u32[]{:S(2)}) %collective-permute-start.11) | collective-permute-done | bytes 221216 | tf_op jit(solution)/shard_map/ppermute | solution.py:24
  120.8 19.9 %collective-permute-done.13 = f16[96,1152]{1,0:T(8,128)(2,1)S(1)} collective-permute-done((f16[96,1152]{1,0:T(8,128)(2,1)S(1)}, f16[96,1152]{1,0:T(8,128)(2,1)S(1)}, u32[]{:S(2)}, u32[]{:S(2)}) %collective-permute-start.13) | collective-permute-done | bytes 221216 | tf_op jit(solution)/shard_map/ppermute | solution.py:24
  (39 shorter events, 11.8 us)
Async XLA Ops:
  6.5 55.5 %all-gather.2.cloned.1.call-start = ((), (), s32[]{:S(2)}) async-start(), calls=%async_computation | async-start | bytes 3932160 | tf_op jit(solution)/shard_map/all_gather | solution.py:166
  7.3 25.6 %collective-permute-start.3 = (bf16[1136,128]{1,0:T(8,128)(2,1)}, bf16[1136,128]{1,0:T(8,128)(2,1)S(1)}, u32[]{:S(2)}, u32[]{:S(2)}) collective-permute-start(bf16[1136,128]{1,0:T(8,128)(2,1)} %bitcast.14), channel_id=1, source_target_pairs={{0,256},{1,257},{2,258},{3,259},{4,260},{5,261},{6,262},{7,263},{8... | collective-permute-start | bytes 872456 | tf_op jit(solution)/shard_map/ppermute | solution.py:24
  23.6 10.8 %collective-permute-start = (bf16[1136,128]{1,0:T(8,128)(2,1)}, bf16[1136,128]{1,0:T(8,128)(2,1)S(1)}, u32[]{:S(2)}, u32[]{:S(2)}) collective-permute-start(bf16[1136,128]{1,0:T(8,128)(2,1)} %bitcast.15), channel_id=1, source_target_pairs={{0,192},{1,193},{2,194},{3,195},{4,196},{5,197},{6,198},{7,199},{8... | collective-permute-start | bytes 872456 | tf_op jit(solution)/shard_map/ppermute | solution.py:24
  28.0 10.8 %collective-permute-start.1 = (bf16[1136,128]{1,0:T(8,128)(2,1)}, bf16[1136,128]{1,0:T(8,128)(2,1)S(1)}, u32[]{:S(2)}, u32[]{:S(2)}) collective-permute-start(bf16[1136,128]{1,0:T(8,128)(2,1)} %bitcast.16), channel_id=1, source_target_pairs={{0,128},{1,129},{2,130},{3,131},{4,132},{5,133},{6,134},{7,135},{8... | collective-permute-start | bytes 872456 | tf_op jit(solution)/shard_map/ppermute | solution.py:24
  30.4 16.4 %collective-permute-start.2 = (bf16[1136,128]{1,0:T(8,128)(2,1)}, bf16[1136,128]{1,0:T(8,128)(2,1)S(1)}, u32[]{:S(2)}, u32[]{:S(2)}) collective-permute-start(bf16[1136,128]{1,0:T(8,128)(2,1)} %bitcast.17), channel_id=1, source_target_pairs={{0,64},{1,65},{2,66},{3,67},{4,68},{5,69},{6,70},{7,71},{8,72},{9,... | collective-permute-start | bytes 872456 | tf_op jit(solution)/shard_map/ppermute | solution.py:24
  46.8 19.2 %collective-permute-start.5 = (bf16[1136,128]{1,0:T(8,128)(2,1)S(1)}, bf16[1136,128]{1,0:T(8,128)(2,1)S(1)}, u32[]{:S(2)}, u32[]{:S(2)}) collective-permute-start(bf16[1136,128]{1,0:T(8,128)(2,1)S(1)} %collective-permute-done.3), channel_id=1, source_target_pairs={{0,192},{1,193},{2,194},{3,195},{4,196},{5,197},{6,198},{7,199},{8... | collective-permute-start | bytes 872456 | tf_op jit(solution)/shard_map/ppermute | solution.py:24
  48.7 17.3 %collective-permute-start.6 = (bf16[1136,128]{1,0:T(8,128)(2,1)S(1)}, bf16[1136,128]{1,0:T(8,128)(2,1)S(1)}, u32[]{:S(2)}, u32[]{:S(2)}) collective-permute-start(bf16[1136,128]{1,0:T(8,128)(2,1)S(1)} %collective-permute-done.3), channel_id=1, source_target_pairs={{0,128},{1,129},{2,130},{3,131},{4,132},{5,133},{6,134},{7,135},{8... | collective-permute-start | bytes 872456 | tf_op jit(solution)/shard_map/ppermute | solution.py:24
  51.0 16.1 %collective-permute-start.7 = (bf16[1136,128]{1,0:T(8,128)(2,1)S(1)}, bf16[1136,128]{1,0:T(8,128)(2,1)S(1)}, u32[]{:S(2)}, u32[]{:S(2)}) collective-permute-start(bf16[1136,128]{1,0:T(8,128)(2,1)S(1)} %collective-permute-done.3), channel_id=1, source_target_pairs={{0,64},{1,65},{2,66},{3,67},{4,68},{5,69},{6,70},{7,71},{8,72},{9,... | collective-permute-start | bytes 872456 | tf_op jit(solution)/shard_map/ppermute | solution.py:24
  55.2 14.5 %collective-permute-start.4 = (bf16[4,1136,128]{2,1,0:T(8,128)(2,1)S(1)}, bf16[4,1136,128]{2,1,0:T(8,128)(2,1)S(1)}, u32[]{:S(2)}, u32[]{:S(2)}) collective-permute-start(bf16[4,1136,128]{2,1,0:T(8,128)(2,1)S(1)} %pad_maximum_fusion.s0), channel_id=1, source_target_pairs={{0,32},{1,33},{2,34},{3,35},{4,36},{5,37},{6,38},{7,39},{8,40},{9,... | collective-permute-start | bytes 3489800 | tf_op jit(solution)/shard_map/ppermute | solution.py:24
  62.0 1.9 %copy-start = (bf16[2048,768]{1,0:T(8,128)(2,1)S(1)}, bf16[2048,768]{1,0:T(8,128)(2,1)}, u32[]{:S(2)}) copy-start(bf16[2048,768]{1,0:T(8,128)(2,1)} %all-gather.2.cloned.1.call-done.all_ref) | copy-start | bytes 9437188
  67.3 6.0 %collective-permute-start.8 = (bf16[4,1136,128]{2,1,0:T(8,128)(2,1)S(1)}, bf16[4,1136,128]{2,1,0:T(8,128)(2,1)S(1)}, u32[]{:S(2)}, u32[]{:S(2)}) collective-permute-start(bf16[4,1136,128]{2,1,0:T(8,128)(2,1)S(1)} %pad_maximum_fusion.1.s1), channel_id=1, source_target_pairs={{0,32},{1,33},{2,34},{3,35},{4,36},{5,37},{6,38},{7,39},{8,40},{9,... | collective-permute-start | bytes 3489800 | tf_op jit(solution)/shard_map/ppermute | solution.py:24
  77.2 17.5 %collective-permute-start.10 = (f16[192,1152]{1,0:T(8,128)(2,1)S(1)}, f16[192,1152]{1,0:T(8,128)(2,1)S(1)}, u32[]{:S(2)}, u32[]{:S(2)}) collective-permute-start(f16[192,1152]{1,0:T(8,128)(2,1)S(1)} %convert_element_type.35), channel_id=1, source_target_pairs={{0,1},{1,0},{2,3},{3,2},{4,5},{5,4},{6,7},{7,6},{8,9},{9,8},{10,11... | collective-permute-start | bytes 1327112 | tf_op jit(solution)/shard_map/ppermute | solution.py:24
  84.3 21.0 %collective-permute-start.9 = (f16[192,1152]{1,0:T(8,128)(2,1)S(1)}, f16[192,1152]{1,0:T(8,128)(2,1)S(1)}, u32[]{:S(2)}, u32[]{:S(2)}) collective-permute-start(f16[192,1152]{1,0:T(8,128)(2,1)S(1)} %convert_element_type.34), channel_id=1, source_target_pairs={{0,1},{1,0},{2,3},{3,2},{4,5},{5,4},{6,7},{7,6},{8,9},{9,8},{10,11... | collective-permute-start | bytes 1327112 | tf_op jit(solution)/shard_map/ppermute | solution.py:24
  95.5 13.9 %collective-permute-start.12 = (f16[96,1152]{1,0:T(8,128)(2,1)S(1)}, f16[96,1152]{1,0:T(8,128)(2,1)S(1)}, u32[]{:S(2)}, u32[]{:S(2)}) collective-permute-start(f16[96,1152]{1,0:T(8,128)(2,1)S(1)} %get-tuple-element.66), channel_id=1, source_target_pairs={{0,2},{1,3},{2,0},{3,1},{4,6},{5,7},{6,4},{7,5},{8,10},{9,11},{10,... | collective-permute-start | bytes 663560 | tf_op jit(solution)/shard_map/ppermute | solution.py:24
  109.9 10.5 %collective-permute-start.11 = (f16[96,1152]{1,0:T(8,128)(2,1)S(1)}, f16[96,1152]{1,0:T(8,128)(2,1)S(1)}, u32[]{:S(2)}, u32[]{:S(2)}) collective-permute-start(f16[96,1152]{1,0:T(8,128)(2,1)S(1)} %get-tuple-element.68), channel_id=1, source_target_pairs={{0,2},{1,3},{2,0},{3,1},{4,6},{5,7},{6,4},{7,5},{8,10},{9,11},{10,... | collective-permute-start | bytes 663560 | tf_op jit(solution)/shard_map/ppermute | solution.py:24
  113.5 27.2 %collective-permute-start.13 = (f16[96,1152]{1,0:T(8,128)(2,1)S(1)}, f16[96,1152]{1,0:T(8,128)(2,1)S(1)}, u32[]{:S(2)}, u32[]{:S(2)}) collective-permute-start(f16[96,1152]{1,0:T(8,128)(2,1)S(1)} %get-tuple-element.74), channel_id=1, source_target_pairs={{0,4},{1,5},{2,6},{3,7},{4,0},{5,1},{6,2},{7,3},{8,12},{9,13},{10,... | collective-permute-start | bytes 663560 | tf_op jit(solution)/shard_map/ppermute | solution.py:24
Sparse Core Ops, SparseCore 0:
  9.5 52.5 all-gather.1

commit v2 on v1

--- a/solution.py
+++ b/solution.py
@@ -115,47 +115,65 @@
             lax.dot_general(grads_ref[j], acts_ref[lo:hi, j * 512:(j + 1) * 512], NT, preferred_element_type=f32) for j in range(2))
 
 
-def rest_kernel(at_ref, s1, t1, grads_ref, start_ref, far_ref, near_ref, keep_far_ref, keep_near_ref, acts_ref, sems):
+def rest_kernel(at_ref, s1, t1, grads_ref, start_ref, *refs):
+    far0_ref, far1_ref, near0_ref, near1_ref, keep_far_ref, keep_near_ref, acts_ref, sems = refs
     for copy in spread(at_ref, s1, t1, acts_ref, sems):
         copy.wait()
+    sends = (far0_ref, far1_ref, near0_ref, near1_ref)
     top = None
     for lo, hi in TILES:
         part = start_ref[:, lo:hi] + sum(
             lax.dot_general(grads_ref[2 + j], acts_ref[lo:hi, j * 512:(j + 1) * 512], NT, preferred_element_type=f32) for j in range(2))
-        far_ref[:, lo:hi] = part[:192]
+        for ref, first in zip(sends, (0, 96, 384, 480)):
+            ref[:, lo:hi] = part[first:first + 96]
         keep_far_ref[:, lo:hi] = part[192:384]
-        near_ref[:, lo:hi] = part[384:576]
         keep_near_ref[:, lo:hi] = part[576:]
         part = jnp.max(jnp.abs(part), axis=0, keepdims=True)
         part = jnp.max(part, axis=1, keepdims=True)
         top = part if top is None else jnp.maximum(top, part)
     size = jnp.clip(jnp.ceil(jnp.log2(top)) + 1, -100, 100)
     scale = jnp.exp2(15 - size)
-    for ref in (far_ref, near_ref):
+    for ref in sends:
         ref[:, :1136] = ref[:, :1136] * scale
-    for ref in (far_ref, near_ref, keep_far_ref, keep_near_ref):
-        ref[:, 1136:] = jnp.broadcast_to(size, (192, 16))
-
-
-def add(keep, message):
-    message = message.astype(f32)
+    for ref in (*sends, keep_far_ref, keep_near_ref):
+        ref[:, 1136:] = jnp.broadcast_to(size, (ref.shape[0], 16))
+
+
+def stage_kernel(spans, keep_ref, message_ref, *out_refs):
+    message = message_ref[...]
     size = message[:, 1136:1137]
-    total = keep + message * jnp.exp2(size - 15)
-    return total, jnp.maximum(keep[:, 1136:1137], size) + 1
-
-
-def tagged(total, size, scale):
-    return jnp.where(lax.broadcasted_iota(jnp.int32, total.shape, 1) < 1136, total * scale, size)
-
-
-def wrap(total, size):
-    return tagged(total, size, jnp.exp2(15 - size)).astype(f16)
+    total = keep_ref[...] + message * jnp.exp2(size - 15)
+    size = jnp.maximum(keep_ref[:, 1136:1137], size) + 1
+    lane = lax.broadcasted_iota(jnp.int32, total.shape, 1)
+    kept = jnp.where(lane < 1136, total, size)
+    sent = jnp.where(lane < 1136, total * jnp.exp2(15 - size), size)
+    for (first, rows, scaled), ref in zip(spans, out_refs):
+        ref[...] = (sent if scaled else kept)[first:first + rows]
+
+
+def stage(keep, message, *spans):
+    return pl.pallas_call(
+        functools.partial(stage_kernel, spans), out_shape=tuple(shape((rows, 1152), f32) for _, rows, _ in spans),
+        in_specs=[VM] * 2, out_specs=(VM,) * len(spans), compiler_params=PARAMS, name="stage",
+    )(keep, message.astype(f32))
+
+
+def final_kernel(n0_ref, n1_ref, c0_ref, c1_ref, out_ref):
+    messages = []
+    for ref in (c0_ref, c1_ref):
+        message = ref[...]
+        messages.append(message * jnp.exp2(message[:, 1136:1137] - 15))
+    near = jnp.concatenate([n0_ref[...], n1_ref[...]], axis=0)
+    out_ref[...] = (near + jnp.concatenate(messages, axis=0))[:, :1136]
 
 
 def again(token):
     return pl.pallas_call(
         fence_kernel, out_shape=shape((8, 128), f32), in_specs=[VM], out_specs=VM, compiler_params=PARAMS, name="fence",
     )(token)
+
+
+FIRST = 64
 
 
 def body(activations, out_grads):
@@ -188,21 +206,24 @@
         scratch_shapes=[pltpu.VMEM((1136, 1024), bf16), pltpu.SemaphoreType.DMA((8,))],
     )(where, s0, t0, grads, token)
     t1, start = tie(t1, start)
-    far, near, keep_far, keep_near = pl.pallas_call(
-        rest_kernel, out_shape=(shape((192, 1152), f32),) * 4,
-        in_specs=[SM] + [ANY] * 2 + [VM] * 2, out_specs=(VM,) * 4, compiler_params=PARAMS, name="rest",
+    *sends, keep_far, keep_near = pl.pallas_call(
+        rest_kernel, out_shape=(shape((96, 1152), f32),) * 4 + (shape((192, 1152), f32),) * 2,
+        in_specs=[SM] + [ANY] * 2 + [VM] * 2, out_specs=(VM,) * 6, compiler_params=PARAMS, name="rest",
         scratch_shapes=[pltpu.VMEM((1136, 1024), bf16), pltpu.SemaphoreType.DMA((8,))],
     )(where, s1, t1, grads, start)
-    f1, n1 = depth_pair(far.astype(f16), 1), depth_pair(near.astype(f16), 1)
-    far, size = add(keep_far, f1)
-    f2 = depth_pair(wrap(far[:96], size[:96]), 2)
-    n1, far = tie(n1, tagged(far[96:], size[96:], 1))
-    near, size = add(keep_near, n1)
-    n2 = depth_pair(wrap(near[:96], size[:96]), 2)
-    crossed = depth_pair(wrap(*add(far, f2)), 4)
-    near, size = add(tagged(near[96:], size[96:], 1), n2)
-    near, crossed = tie(tagged(near, size, 1), crossed)
-    return add(near, crossed)[0][:, :1136]
+    f0, f1, n0, n1 = (depth_pair(m.astype(f16), 1) for m in sends)
+    f2 = stage(keep_far[:96], f0, (0, FIRST, True), (FIRST, 96 - FIRST, True))
+    f2 = [depth_pair(m.astype(f16), 2) for m in f2]
+    k0, k1 = stage(keep_far[96:], f1, (0, FIRST, False), (FIRST, 96 - FIRST, False))
+    n2 = stage(keep_near[:96], n0, (0, 48, True), (48, 48, True))
+    n2 = [depth_pair(m.astype(f16), 2) for m in n2]
+    crossed = [depth_pair(stage(k, m, (0, k.shape[0], True))[0].astype(f16), 4) for k, m in zip((k0, k1), f2)]
+    n0, n1 = stage(keep_near[96:], n1, (0, 48, False), (48, 48, False))
+    near = [stage(k, m, (0, 48, False))[0] for k, m in zip((n0, n1), n2)]
+    *near, c0, c1 = tie(*near, *crossed)
+    return pl.pallas_call(
+        final_kernel, out_shape=shape((96, 1136), f32), in_specs=[VM] * 4, out_specs=VM, compiler_params=PARAMS, name="final",
+    )(*near, c0.astype(f32), c1.astype(f32))
 
 
 def solution(mesh):

time: 149 us -> 140 us (0.940)
  the two profiles are of different devices: /device:TPU:1 before, /device:TPU:43 now
where the time goes in v2:
time: 140 us
  starting transfers between devices  76 us (54%)
  waiting for transfers between devices  34.7 us (25%)
  between operations  13.9 us (10%)
  Pallas kernels  11.2 us (8%)
  local copies, waits for them, and re-layouts  2.09 us (1%)
  other arithmetic  1.68 us (1%)
    ppermute x19, starting transfers between devices, permute(): return lax.ppermute(value, AXES, pairs)  76 us
    ppermute x19, waiting for transfers between devices, permute(): return lax.ppermute(value, AXES, pairs)  34 us
    pallas_call x1, Pallas kernels, body(): pl.pallas_call(rest_kernel, out_shape=(shape((96, 1152), f32),) * 4 + (sh...  3.8 us
    pallas_call x1, Pallas kernels, body(): pl.pallas_call(own_kernel, out_shape=shape((768, 1136), f32), in_specs=[S...  3.55 us
  transfers between devices with their start and end apart: 20, of which 6 were waited for; matrix products, arithmetic and copies ran while one was open for 1% of the time, Pallas kernels for 5%

profile of v2, /device:TPU:43, one launch (start us, length us, event | category | flops | bytes accessed | tf_op | source)
XLA Modules:
  0.0 139.6 jit_solution(14712824424407798442)
XLA Ops:
  7.3 14.5 %collective-permute-start.3 = (bf16[1136,128]{1,0:T(8,128)(2,1)}, bf16[1136,128]{1,0:T(8,128)(2,1)S(1)}, u32[]{:S(2)}, u32[]{:S(2)}) collective-permute-start(bf16[1136,128]{1,0:T(8,128)(2,1)} %bitcast.14), channel_id=1, source_target_pairs={{0,256},{1,257},{2,258},{3,259},{4,260},{5,261},{6,262},{7,263},{8... | collective-permute-start | bytes 872456 | tf_op jit(solution)/shard_map/ppermute | solution.py:24
  21.8 3.1 %collective-permute-start.2 = (bf16[1136,128]{1,0:T(8,128)(2,1)}, bf16[1136,128]{1,0:T(8,128)(2,1)S(1)}, u32[]{:S(2)}, u32[]{:S(2)}) collective-permute-start(bf16[1136,128]{1,0:T(8,128)(2,1)} %bitcast.15), channel_id=1, source_target_pairs={{0,64},{1,65},{2,66},{3,67},{4,68},{5,69},{6,70},{7,71},{8,72},{9,... | collective-permute-start | bytes 872456 | tf_op jit(solution)/shard_map/ppermute | solution.py:24
  25.0 2.7 %collective-permute-start.1 = (bf16[1136,128]{1,0:T(8,128)(2,1)}, bf16[1136,128]{1,0:T(8,128)(2,1)S(1)}, u32[]{:S(2)}, u32[]{:S(2)}) collective-permute-start(bf16[1136,128]{1,0:T(8,128)(2,1)} %bitcast.16), channel_id=1, source_target_pairs={{0,128},{1,129},{2,130},{3,131},{4,132},{5,133},{6,134},{7,135},{8... | collective-permute-start | bytes 872456 | tf_op jit(solution)/shard_map/ppermute | solution.py:24
  27.7 3.8 %collective-permute-start = (bf16[1136,128]{1,0:T(8,128)(2,1)}, bf16[1136,128]{1,0:T(8,128)(2,1)S(1)}, u32[]{:S(2)}, u32[]{:S(2)}) collective-permute-start(bf16[1136,128]{1,0:T(8,128)(2,1)} %bitcast.17), channel_id=1, source_target_pairs={{0,192},{1,193},{2,194},{3,195},{4,196},{5,197},{6,198},{7,199},{8... | collective-permute-start | bytes 872456 | tf_op jit(solution)/shard_map/ppermute | solution.py:24
  31.5 15.4 %collective-permute-done.3 = bf16[1136,128]{1,0:T(8,128)(2,1)S(1)} collective-permute-done((bf16[1136,128]{1,0:T(8,128)(2,1)}, bf16[1136,128]{1,0:T(8,128)(2,1)S(1)}, u32[]{:S(2)}, u32[]{:S(2)}) %collective-permute-start.3) | collective-permute-done | bytes 290848 | tf_op jit(solution)/shard_map/ppermute | solution.py:24
  46.9 3.1 %collective-permute-start.7 = (bf16[1136,128]{1,0:T(8,128)(2,1)S(1)}, bf16[1136,128]{1,0:T(8,128)(2,1)S(1)}, u32[]{:S(2)}, u32[]{:S(2)}) collective-permute-start(bf16[1136,128]{1,0:T(8,128)(2,1)S(1)} %collective-permute-done.3), channel_id=1, source_target_pairs={{0,64},{1,65},{2,66},{3,67},{4,68},{5,69},{6,70},{7,71},{8,72},{9,... | collective-permute-start | bytes 872456 | tf_op jit(solution)/shard_map/ppermute | solution.py:24
  50.0 2.7 %collective-permute-start.6 = (bf16[1136,128]{1,0:T(8,128)(2,1)S(1)}, bf16[1136,128]{1,0:T(8,128)(2,1)S(1)}, u32[]{:S(2)}, u32[]{:S(2)}) collective-permute-start(bf16[1136,128]{1,0:T(8,128)(2,1)S(1)} %collective-permute-done.3), channel_id=1, source_target_pairs={{0,128},{1,129},{2,130},{3,131},{4,132},{5,133},{6,134},{7,135},{8... | collective-permute-start | bytes 872456 | tf_op jit(solution)/shard_map/ppermute | solution.py:24
  52.8 3.8 %collective-permute-start.5 = (bf16[1136,128]{1,0:T(8,128)(2,1)S(1)}, bf16[1136,128]{1,0:T(8,128)(2,1)S(1)}, u32[]{:S(2)}, u32[]{:S(2)}) collective-permute-start(bf16[1136,128]{1,0:T(8,128)(2,1)S(1)} %collective-permute-done.3), channel_id=1, source_target_pairs={{0,192},{1,193},{2,194},{3,195},{4,196},{5,197},{6,198},{7,199},{8... | collective-permute-start | bytes 872456 | tf_op jit(solution)/shard_map/ppermute | solution.py:24
  57.8 4.3 %collective-permute-start.4 = (bf16[4,1136,128]{2,1,0:T(8,128)(2,1)S(1)}, bf16[4,1136,128]{2,1,0:T(8,128)(2,1)S(1)}, u32[]{:S(2)}, u32[]{:S(2)}) collective-permute-start(bf16[4,1136,128]{2,1,0:T(8,128)(2,1)S(1)} %pad_maximum_fusion.s0), channel_id=1, source_target_pairs={{0,32},{1,33},{2,34},{3,35},{4,36},{5,37},{6,38},{7,39},{8,40},{9,... | collective-permute-start | bytes 3489800 | tf_op jit(solution)/shard_map/ppermute | solution.py:24
  64.0 2.0 %prep.1.grads_ref = bf16[4,768,512]{2,1,0:T(8,128)(2,1)S(1)} custom-call(s32[5]{0:T(128)S(1)} %stack.53.at_ref, bf16[2048,768]{1,0:T(8,128)(2,1)S(1)} %copy-done), custom_call_target="tpu_custom_call" | custom-call | tf_op jit(solution)/shard_map/prep/pallas_call | solution.py:194
  66.1 2.4 %collective-permute-done.5 = bf16[1136,128]{1,0:T(8,128)(2,1)S(1)} collective-permute-done((bf16[1136,128]{1,0:T(8,128)(2,1)S(1)}, bf16[1136,128]{1,0:T(8,128)(2,1)S(1)}, u32[]{:S(2)}, u32[]{:S(2)}) %collective-permute-start.5) | collective-permute-done | bytes 290848 | tf_op jit(solution)/shard_map/ppermute | solution.py:24
  68.7 2.4 %collective-permute-start.8 = (bf16[4,1136,128]{2,1,0:T(8,128)(2,1)S(1)}, bf16[4,1136,128]{2,1,0:T(8,128)(2,1)S(1)}, u32[]{:S(2)}, u32[]{:S(2)}) collective-permute-start(bf16[4,1136,128]{2,1,0:T(8,128)(2,1)S(1)} %pad_maximum_fusion.1.s1), channel_id=1, source_target_pairs={{0,32},{1,33},{2,34},{3,35},{4,36},{5,37},{6,38},{7,39},{8,40},{9,... | collective-permute-start | bytes 3489800 | tf_op jit(solution)/shard_map/ppermute | solution.py:24
  71.1 3.6 %own.1.start_ref = f32[768,1136]{1,0:T(8,128)S(1)} custom-call(s32[5]{0:T(128)S(1)} %stack.53.at_ref, bf16[4,1136,128]{2,1,0:T(8,128)(2,1)S(1)} %pad_maximum_fusion.s0, bf16[4,1136,128]{2,1,0:T(8,128)(2,1)S(1)} %collective-permute-done.4.t0, bf16[4,768,512]{2,1,0:T(8,128)(2,1)S(1)} %prep.1.grads_ref, f32[8,128]{1,0:T(8,128)S(1)} %fence.3.token), custom_call_target="tpu_custom_call" | custom-call | tf_op jit(solution)/shard_map/own/pallas_call | solution.py:203
  74.7 3.8 %rest.1 = (f32[96,1152]{1,0:T(8,128)S(1)}, f32[96,1152]{1,0:T(8,128)S(1)}, f32[96,1152]{1,0:T(8,128)S(1)}, f32[96,1152]{1,0:T(8,128)S(1)}, f32[192,1152]{1,0:T(8,128)S(1)}, /*index=5*/f32[192,1152]{1,0:T(8,128)S(1)}) custom-call(s32[5]{0:T(128)S(1)} %stack.53.at_ref, bf16[4,1136,128]{2,1,0:T(8,128)(2,1)S(1)} %pad_maximum_fusion.1.s1, ...), custom_call_target="tpu_custom_call" | custom-call | tf_op jit(solution)/shard_map/rest/pallas_call | solution.py:209
  78.6 1.9 %collective-permute-start.14 = (f16[96,1152]{1,0:T(8,128)(2,1)S(1)}, f16[96,1152]{1,0:T(8,128)(2,1)S(1)}, u32[]{:S(2)}, u32[]{:S(2)}) collective-permute-start(f16[96,1152]{1,0:T(8,128)(2,1)S(1)} %convert_element_type.74), channel_id=1, source_target_pairs={{0,1},{1,0},{2,3},{3,2},{4,5},{5,4},{6,7},{7,6},{8,9},{9,8},{10,11... | collective-permute-start | bytes 663560 | tf_op jit(solution)/shard_map/ppermute | solution.py:24
  80.5 3.4 %collective-permute-start.13 = (f16[96,1152]{1,0:T(8,128)(2,1)S(1)}, f16[96,1152]{1,0:T(8,128)(2,1)S(1)}, u32[]{:S(2)}, u32[]{:S(2)}) collective-permute-start(f16[96,1152]{1,0:T(8,128)(2,1)S(1)} %convert_element_type.72), channel_id=1, source_target_pairs={{0,1},{1,0},{2,3},{3,2},{4,5},{5,4},{6,7},{7,6},{8,9},{9,8},{10,11... | collective-permute-start | bytes 663560 | tf_op jit(solution)/shard_map/ppermute | solution.py:24
  89.7 2.1 %collective-permute-start.9 = (f16[96,1152]{1,0:T(8,128)(2,1)S(1)}, f16[96,1152]{1,0:T(8,128)(2,1)S(1)}, u32[]{:S(2)}, u32[]{:S(2)}) collective-permute-start(f16[96,1152]{1,0:T(8,128)(2,1)S(1)} %convert_element_type.64), channel_id=1, source_target_pairs={{0,1},{1,0},{2,3},{3,2},{4,5},{5,4},{6,7},{7,6},{8,9},{9,8},{10,11... | collective-permute-start | bytes 663560 | tf_op jit(solution)/shard_map/ppermute | solution.py:24
  91.8 4.3 %collective-permute-start.17 = (f16[32,1152]{1,0:T(8,128)(2,1)S(1)}, f16[32,1152]{1,0:T(8,128)(2,1)S(1)}, u32[]{:S(2)}, u32[]{:S(2)}) collective-permute-start(f16[32,1152]{1,0:T(8,128)(2,1)S(1)} %convert_element_type.79), channel_id=1, source_target_pairs={{0,2},{1,3},{2,0},{3,1},{4,6},{5,7},{6,4},{7,5},{8,10},{9,11},{10,... | collective-permute-start | bytes 221192 | tf_op jit(solution)/shard_map/ppermute | solution.py:24
  96.5 11.9 %collective-permute-start.16 = (f16[64,1152]{1,0:T(8,128)(2,1)S(1)}, f16[64,1152]{1,0:T(8,128)(2,1)S(1)}, u32[]{:S(2)}, u32[]{:S(2)}) collective-permute-start(f16[64,1152]{1,0:T(8,128)(2,1)S(1)} %convert_element_type.78), channel_id=1, source_target_pairs={{0,4},{1,5},{2,6},{3,7},{4,0},{5,1},{6,2},{7,3},{8,12},{9,13},{10,... | collective-permute-start | bytes 442376 | tf_op jit(solution)/shard_map/ppermute | solution.py:24
  108.6 1.9 %collective-permute-start.11 = (f16[48,1152]{1,0:T(8,128)(2,1)S(1)}, f16[48,1152]{1,0:T(8,128)(2,1)S(1)}, u32[]{:S(2)}, u32[]{:S(2)}) collective-permute-start(f16[48,1152]{1,0:T(8,128)(2,1)S(1)} %convert_element_type.68), channel_id=1, source_target_pairs={{0,2},{1,3},{2,0},{3,1},{4,6},{5,7},{6,4},{7,5},{8,10},{9,11},{10,... | collective-permute-start | bytes 331784 | tf_op jit(solution)/shard_map/ppermute | solution.py:24
  110.6 4.3 %collective-permute-start.12 = (f16[48,1152]{1,0:T(8,128)(2,1)S(1)}, f16[48,1152]{1,0:T(8,128)(2,1)S(1)}, u32[]{:S(2)}, u32[]{:S(2)}) collective-permute-start(f16[48,1152]{1,0:T(8,128)(2,1)S(1)} %convert_element_type.70), channel_id=1, source_target_pairs={{0,2},{1,3},{2,0},{3,1},{4,6},{5,7},{6,4},{7,5},{8,10},{9,11},{10,... | collective-permute-start | bytes 331784 | tf_op jit(solution)/shard_map/ppermute | solution.py:24
  117.1 3.9 %collective-permute-done.11 = f16[48,1152]{1,0:T(8,128)(2,1)S(1)} collective-permute-done((f16[48,1152]{1,0:T(8,128)(2,1)S(1)}, f16[48,1152]{1,0:T(8,128)(2,1)S(1)}, u32[]{:S(2)}, u32[]{:S(2)}) %collective-permute-start.11) | collective-permute-done | bytes 110624 | tf_op jit(solution)/shard_map/ppermute | solution.py:24
  121.1 2.5 %collective-permute-done.12 = f16[48,1152]{1,0:T(8,128)(2,1)S(1)} collective-permute-done((f16[48,1152]{1,0:T(8,128)(2,1)S(1)}, f16[48,1152]{1,0:T(8,128)(2,1)S(1)}, u32[]{:S(2)}, u32[]{:S(2)}) %collective-permute-start.12) | collective-permute-done | bytes 110624 | tf_op jit(solution)/shard_map/ppermute | solution.py:24
  123.7 8.2 %collective-permute-done.18 = f16[32,1152]{1,0:T(8,128)(2,1)S(1)} collective-permute-done((f16[32,1152]{1,0:T(8,128)(2,1)S(1)}, f16[32,1152]{1,0:T(8,128)(2,1)S(1)}, u32[]{:S(2)}, u32[]{:S(2)}) %collective-permute-start.18) | collective-permute-done | bytes 73760 | tf_op jit(solution)/shard_map/ppermute | solution.py:24
  (58 shorter events, 13.7 us)
Async XLA Ops:
  6.5 55.6 %all-gather.2.cloned.1.call-start = ((), (), s32[]{:S(2)}) async-start(), calls=%async_computation | async-start | bytes 3932160 | tf_op jit(solution)/shard_map/all_gather | solution.py:184
  7.3 39.6 %collective-permute-start.3 = (bf16[1136,128]{1,0:T(8,128)(2,1)}, bf16[1136,128]{1,0:T(8,128)(2,1)S(1)}, u32[]{:S(2)}, u32[]{:S(2)}) collective-permute-start(bf16[1136,128]{1,0:T(8,128)(2,1)} %bitcast.14), channel_id=1, source_target_pairs={{0,256},{1,257},{2,258},{3,259},{4,260},{5,261},{6,262},{7,263},{8... | collective-permute-start | bytes 872456 | tf_op jit(solution)/shard_map/ppermute | solution.py:24
  21.8 25.1 %collective-permute-start.2 = (bf16[1136,128]{1,0:T(8,128)(2,1)}, bf16[1136,128]{1,0:T(8,128)(2,1)S(1)}, u32[]{:S(2)}, u32[]{:S(2)}) collective-permute-start(bf16[1136,128]{1,0:T(8,128)(2,1)} %bitcast.15), channel_id=1, source_target_pairs={{0,64},{1,65},{2,66},{3,67},{4,68},{5,69},{6,70},{7,71},{8,72},{9,... | collective-permute-start | bytes 872456 | tf_op jit(solution)/shard_map/ppermute | solution.py:24
  25.0 21.9 %collective-permute-start.1 = (bf16[1136,128]{1,0:T(8,128)(2,1)}, bf16[1136,128]{1,0:T(8,128)(2,1)S(1)}, u32[]{:S(2)}, u32[]{:S(2)}) collective-permute-start(bf16[1136,128]{1,0:T(8,128)(2,1)} %bitcast.16), channel_id=1, source_target_pairs={{0,128},{1,129},{2,130},{3,131},{4,132},{5,133},{6,134},{7,135},{8... | collective-permute-start | bytes 872456 | tf_op jit(solution)/shard_map/ppermute | solution.py:24
  27.7 19.2 %collective-permute-start = (bf16[1136,128]{1,0:T(8,128)(2,1)}, bf16[1136,128]{1,0:T(8,128)(2,1)S(1)}, u32[]{:S(2)}, u32[]{:S(2)}) collective-permute-start(bf16[1136,128]{1,0:T(8,128)(2,1)} %bitcast.17), channel_id=1, source_target_pairs={{0,192},{1,193},{2,194},{3,195},{4,196},{5,197},{6,198},{7,199},{8... | collective-permute-start | bytes 872456 | tf_op jit(solution)/shard_map/ppermute | solution.py:24
  46.9 19.2 %collective-permute-start.7 = (bf16[1136,128]{1,0:T(8,128)(2,1)S(1)}, bf16[1136,128]{1,0:T(8,128)(2,1)S(1)}, u32[]{:S(2)}, u32[]{:S(2)}) collective-permute-start(bf16[1136,128]{1,0:T(8,128)(2,1)S(1)} %collective-permute-done.3), channel_id=1, source_target_pairs={{0,64},{1,65},{2,66},{3,67},{4,68},{5,69},{6,70},{7,71},{8,72},{9,... | collective-permute-start | bytes 872456 | tf_op jit(solution)/shard_map/ppermute | solution.py:24
  50.0 16.0 %collective-permute-start.6 = (bf16[1136,128]{1,0:T(8,128)(2,1)S(1)}, bf16[1136,128]{1,0:T(8,128)(2,1)S(1)}, u32[]{:S(2)}, u32[]{:S(2)}) collective-permute-start(bf16[1136,128]{1,0:T(8,128)(2,1)S(1)} %collective-permute-done.3), channel_id=1, source_target_pairs={{0,128},{1,129},{2,130},{3,131},{4,132},{5,133},{6,134},{7,135},{8... | collective-permute-start | bytes 872456 | tf_op jit(solution)/shard_map/ppermute | solution.py:24
  52.8 15.7 %collective-permute-start.5 = (bf16[1136,128]{1,0:T(8,128)(2,1)S(1)}, bf16[1136,128]{1,0:T(8,128)(2,1)S(1)}, u32[]{:S(2)}, u32[]{:S(2)}) collective-permute-start(bf16[1136,128]{1,0:T(8,128)(2,1)S(1)} %collective-permute-done.3), channel_id=1, source_target_pairs={{0,192},{1,193},{2,194},{3,195},{4,196},{5,197},{6,198},{7,199},{8... | collective-permute-start | bytes 872456 | tf_op jit(solution)/shard_map/ppermute | solution.py:24
  57.8 13.3 %collective-permute-start.4 = (bf16[4,1136,128]{2,1,0:T(8,128)(2,1)S(1)}, bf16[4,1136,128]{2,1,0:T(8,128)(2,1)S(1)}, u32[]{:S(2)}, u32[]{:S(2)}) collective-permute-start(bf16[4,1136,128]{2,1,0:T(8,128)(2,1)S(1)} %pad_maximum_fusion.s0), channel_id=1, source_target_pairs={{0,32},{1,33},{2,34},{3,35},{4,36},{5,37},{6,38},{7,39},{8,40},{9,... | collective-permute-start | bytes 3489800 | tf_op jit(solution)/shard_map/ppermute | solution.py:24
  62.1 1.9 %copy-start = (bf16[2048,768]{1,0:T(8,128)(2,1)S(1)}, bf16[2048,768]{1,0:T(8,128)(2,1)}, u32[]{:S(2)}) copy-start(bf16[2048,768]{1,0:T(8,128)(2,1)} %all-gather.2.cloned.1.call-done.all_ref) | copy-start | bytes 9437188
  68.7 6.0 %collective-permute-start.8 = (bf16[4,1136,128]{2,1,0:T(8,128)(2,1)S(1)}, bf16[4,1136,128]{2,1,0:T(8,128)(2,1)S(1)}, u32[]{:S(2)}, u32[]{:S(2)}) collective-permute-start(bf16[4,1136,128]{2,1,0:T(8,128)(2,1)S(1)} %pad_maximum_fusion.1.s1), channel_id=1, source_target_pairs={{0,32},{1,33},{2,34},{3,35},{4,36},{5,37},{6,38},{7,39},{8,40},{9,... | collective-permute-start | bytes 3489800 | tf_op jit(solution)/shard_map/ppermute | solution.py:24
  78.6 8.9 %collective-permute-start.14 = (f16[96,1152]{1,0:T(8,128)(2,1)S(1)}, f16[96,1152]{1,0:T(8,128)(2,1)S(1)}, u32[]{:S(2)}, u32[]{:S(2)}) collective-permute-start(f16[96,1152]{1,0:T(8,128)(2,1)S(1)} %convert_element_type.74), channel_id=1, source_target_pairs={{0,1},{1,0},{2,3},{3,2},{4,5},{5,4},{6,7},{7,6},{8,9},{9,8},{10,11... | collective-permute-start | bytes 663560 | tf_op jit(solution)/shard_map/ppermute | solution.py:24
  80.5 15.6 %collective-permute-start.13 = (f16[96,1152]{1,0:T(8,128)(2,1)S(1)}, f16[96,1152]{1,0:T(8,128)(2,1)S(1)}, u32[]{:S(2)}, u32[]{:S(2)}) collective-permute-start(f16[96,1152]{1,0:T(8,128)(2,1)S(1)} %convert_element_type.72), channel_id=1, source_target_pairs={{0,1},{1,0},{2,3},{3,2},{4,5},{5,4},{6,7},{7,6},{8,9},{9,8},{10,11... | collective-permute-start | bytes 663560 | tf_op jit(solution)/shard_map/ppermute | solution.py:24
  83.9 24.5 %collective-permute-start.10 = (f16[96,1152]{1,0:T(8,128)(2,1)S(1)}, f16[96,1152]{1,0:T(8,128)(2,1)S(1)}, u32[]{:S(2)}, u32[]{:S(2)}) collective-permute-start(f16[96,1152]{1,0:T(8,128)(2,1)S(1)} %convert_element_type.66), channel_id=1, source_target_pairs={{0,1},{1,0},{2,3},{3,2},{4,5},{5,4},{6,7},{7,6},{8,9},{9,8},{10,11... | collective-permute-start | bytes 663560 | tf_op jit(solution)/shard_map/ppermute | solution.py:24
  87.7 8.6 %collective-permute-start.15 = (f16[64,1152]{1,0:T(8,128)(2,1)S(1)}, f16[64,1152]{1,0:T(8,128)(2,1)S(1)}, u32[]{:S(2)}, u32[]{:S(2)}) collective-permute-start(f16[64,1152]{1,0:T(8,128)(2,1)S(1)} %convert_element_type.76), channel_id=1, source_target_pairs={{0,2},{1,3},{2,0},{3,1},{4,6},{5,7},{6,4},{7,5},{8,10},{9,11},{10,... | collective-permute-start | bytes 442376 | tf_op jit(solution)/shard_map/ppermute | solution.py:24
  89.7 27.2 %collective-permute-start.9 = (f16[96,1152]{1,0:T(8,128)(2,1)S(1)}, f16[96,1152]{1,0:T(8,128)(2,1)S(1)}, u32[]{:S(2)}, u32[]{:S(2)}) collective-permute-start(f16[96,1152]{1,0:T(8,128)(2,1)S(1)} %convert_element_type.64), channel_id=1, source_target_pairs={{0,1},{1,0},{2,3},{3,2},{4,5},{5,4},{6,7},{7,6},{8,9},{9,8},{10,11... | collective-permute-start | bytes 663560 | tf_op jit(solution)/shard_map/ppermute | solution.py:24
  91.8 23.0 %collective-permute-start.17 = (f16[32,1152]{1,0:T(8,128)(2,1)S(1)}, f16[32,1152]{1,0:T(8,128)(2,1)S(1)}, u32[]{:S(2)}, u32[]{:S(2)}) collective-permute-start(f16[32,1152]{1,0:T(8,128)(2,1)S(1)} %convert_element_type.79), channel_id=1, source_target_pairs={{0,2},{1,3},{2,0},{3,1},{4,6},{5,7},{6,4},{7,5},{8,10},{9,11},{10,... | collective-permute-start | bytes 221192 | tf_op jit(solution)/shard_map/ppermute | solution.py:24
  96.5 35.4 %collective-permute-start.16 = (f16[64,1152]{1,0:T(8,128)(2,1)S(1)}, f16[64,1152]{1,0:T(8,128)(2,1)S(1)}, u32[]{:S(2)}, u32[]{:S(2)}) collective-permute-start(f16[64,1152]{1,0:T(8,128)(2,1)S(1)} %convert_element_type.78), channel_id=1, source_target_pairs={{0,4},{1,5},{2,6},{3,7},{4,0},{5,1},{6,2},{7,3},{8,12},{9,13},{10,... | collective-permute-start | bytes 442376 | tf_op jit(solution)/shard_map/ppermute | solution.py:24
  108.6 12.4 %collective-permute-start.11 = (f16[48,1152]{1,0:T(8,128)(2,1)S(1)}, f16[48,1152]{1,0:T(8,128)(2,1)S(1)}, u32[]{:S(2)}, u32[]{:S(2)}) collective-permute-start(f16[48,1152]{1,0:T(8,128)(2,1)S(1)} %convert_element_type.68), channel_id=1, source_target_pairs={{0,2},{1,3},{2,0},{3,1},{4,6},{5,7},{6,4},{7,5},{8,10},{9,11},{10,... | collective-permute-start | bytes 331784 | tf_op jit(solution)/shard_map/ppermute | solution.py:24
  110.6 13.0 %collective-permute-start.12 = (f16[48,1152]{1,0:T(8,128)(2,1)S(1)}, f16[48,1152]{1,0:T(8,128)(2,1)S(1)}, u32[]{:S(2)}, u32[]{:S(2)}) collective-permute-start(f16[48,1152]{1,0:T(8,128)(2,1)S(1)} %convert_element_type.70), channel_id=1, source_target_pairs={{0,2},{1,3},{2,0},{3,1},{4,6},{5,7},{6,4},{7,5},{8,10},{9,11},{10,... | collective-permute-start | bytes 331784 | tf_op jit(solution)/shard_map/ppermute | solution.py:24
  115.0 16.9 %collective-permute-start.18 = (f16[32,1152]{1,0:T(8,128)(2,1)S(1)}, f16[32,1152]{1,0:T(8,128)(2,1)S(1)}, u32[]{:S(2)}, u32[]{:S(2)}) collective-permute-start(f16[32,1152]{1,0:T(8,128)(2,1)S(1)} %convert_element_type.81), channel_id=1, source_target_pairs={{0,4},{1,5},{2,6},{3,7},{4,0},{5,1},{6,2},{7,3},{8,12},{9,13},{10,... | collective-permute-start | bytes 221192 | tf_op jit(solution)/shard_map/ppermute | solution.py:24
Sparse Core Ops, SparseCore 0:
  9.5 50.4 all-gather.1

commit v3 on v2

--- a/solution.py
+++ b/solution.py
@@ -158,13 +158,9 @@
     )(keep, message.astype(f32))
 
 
-def final_kernel(n0_ref, n1_ref, c0_ref, c1_ref, out_ref):
-    messages = []
-    for ref in (c0_ref, c1_ref):
-        message = ref[...]
-        messages.append(message * jnp.exp2(message[:, 1136:1137] - 15))
-    near = jnp.concatenate([n0_ref[...], n1_ref[...]], axis=0)
-    out_ref[...] = (near + jnp.concatenate(messages, axis=0))[:, :1136]
+def final_kernel(near_ref, message_ref, out_ref):
+    message = message_ref[...]
+    out_ref[...] = (near_ref[...] + message * jnp.exp2(message[:, 1136:1137] - 15))[:, :1136]
 
 
 def again(token):
@@ -212,18 +208,18 @@
         scratch_shapes=[pltpu.VMEM((1136, 1024), bf16), pltpu.SemaphoreType.DMA((8,))],
     )(where, s1, t1, grads, start)
     f0, f1, n0, n1 = (depth_pair(m.astype(f16), 1) for m in sends)
-    f2 = stage(keep_far[:96], f0, (0, FIRST, True), (FIRST, 96 - FIRST, True))
-    f2 = [depth_pair(m.astype(f16), 2) for m in f2]
-    k0, k1 = stage(keep_far[96:], f1, (0, FIRST, False), (FIRST, 96 - FIRST, False))
-    n2 = stage(keep_near[:96], n0, (0, 48, True), (48, 48, True))
-    n2 = [depth_pair(m.astype(f16), 2) for m in n2]
-    crossed = [depth_pair(stage(k, m, (0, k.shape[0], True))[0].astype(f16), 4) for k, m in zip((k0, k1), f2)]
-    n0, n1 = stage(keep_near[96:], n1, (0, 48, False), (48, 48, False))
-    near = [stage(k, m, (0, 48, False))[0] for k, m in zip((n0, n1), n2)]
-    *near, c0, c1 = tie(*near, *crossed)
+    (f2,) = stage(keep_far[:96], f0, (0, 96, True))
+    f2 = depth_pair(f2.astype(f16), 2)
+    (far,) = stage(keep_far[96:], f1, (0, 96, False))
+    (n2,) = stage(keep_near[:96], n0, (0, 96, True))
+    n2 = depth_pair(n2.astype(f16), 2)
+    crossed = depth_pair(stage(far, f2, (0, 96, True))[0].astype(f16), 4)
+    (near,) = stage(keep_near[96:], n1, (0, 96, False))
+    (near,) = stage(near, n2, (0, 96, False))
+    near, crossed = tie(near, crossed)
     return pl.pallas_call(
-        final_kernel, out_shape=shape((96, 1136), f32), in_specs=[VM] * 4, out_specs=VM, compiler_params=PARAMS, name="final",
-    )(*near, c0.astype(f32), c1.astype(f32))
+        final_kernel, out_shape=shape((96, 1136), f32), in_specs=[VM] * 2, out_specs=VM, compiler_params=PARAMS, name="final",
+    )(near, crossed.astype(f32))
 
 
 def solution(mesh):

time: 140 us -> 138 us (0.986)
  the two profiles are of different devices: /device:TPU:43 before, /device:TPU:2 now
where the time goes in v3:
time: 138 us
  starting transfers between devices  67.6 us (49%)
  waiting for transfers between devices  41.3 us (30%)
  between operations  13.8 us (10%)
  Pallas kernels  11 us (8%)
  local copies, waits for them, and re-layouts  2.1 us (2%)
  other arithmetic  1.67 us (1%)
    ppermute x16, starting transfers between devices, permute(): return lax.ppermute(value, AXES, pairs)  67.6 us
    ppermute x16, waiting for transfers between devices, permute(): return lax.ppermute(value, AXES, pairs)  36.4 us
    all_gather x1, waiting for transfers between devices, body(): every_grad = lax.all_gather(out_grads, 'col', axis=0, tiled=True)  4.17 us
    pallas_call x1, Pallas kernels, body(): pl.pallas_call(rest_kernel, out_shape=(shape((96, 1152), f32),) * 4 + (sh...  3.8 us
    pallas_call x1, Pallas kernels, body(): pl.pallas_call(own_kernel, out_shape=shape((768, 1136), f32), in_specs=[S...  3.55 us
  transfers between devices with their start and end apart: 17, of which 9 were waited for; matrix products, arithmetic and copies ran while one was open for 1% of the time, Pallas kernels for 5%

profile of v3, /device:TPU:2, one launch (start us, length us, event | category | flops | bytes accessed | tf_op | source)
XLA Modules:
  0.0 137.5 jit_solution(18108725922594973568)
XLA Ops:
  7.3 15.7 %collective-permute-start.3 = (bf16[1136,128]{1,0:T(8,128)(2,1)}, bf16[1136,128]{1,0:T(8,128)(2,1)S(1)}, u32[]{:S(2)}, u32[]{:S(2)}) collective-permute-start(bf16[1136,128]{1,0:T(8,128)(2,1)} %bitcast.14), channel_id=1, source_target_pairs={{0,256},{1,257},{2,258},{3,259},{4,260},{5,261},{6,262},{7,263},{8... | collective-permute-start | bytes 872456 | tf_op jit(solution)/shard_map/ppermute | solution.py:24
  23.0 3.4 %collective-permute-start.2 = (bf16[1136,128]{1,0:T(8,128)(2,1)}, bf16[1136,128]{1,0:T(8,128)(2,1)S(1)}, u32[]{:S(2)}, u32[]{:S(2)}) collective-permute-start(bf16[1136,128]{1,0:T(8,128)(2,1)} %bitcast.15), channel_id=1, source_target_pairs={{0,64},{1,65},{2,66},{3,67},{4,68},{5,69},{6,70},{7,71},{8,72},{9,... | collective-permute-start | bytes 872456 | tf_op jit(solution)/shard_map/ppermute | solution.py:24
  26.4 3.0 %collective-permute-start.1 = (bf16[1136,128]{1,0:T(8,128)(2,1)}, bf16[1136,128]{1,0:T(8,128)(2,1)S(1)}, u32[]{:S(2)}, u32[]{:S(2)}) collective-permute-start(bf16[1136,128]{1,0:T(8,128)(2,1)} %bitcast.16), channel_id=1, source_target_pairs={{0,128},{1,129},{2,130},{3,131},{4,132},{5,133},{6,134},{7,135},{8... | collective-permute-start | bytes 872456 | tf_op jit(solution)/shard_map/ppermute | solution.py:24
  29.5 4.1 %collective-permute-start = (bf16[1136,128]{1,0:T(8,128)(2,1)}, bf16[1136,128]{1,0:T(8,128)(2,1)S(1)}, u32[]{:S(2)}, u32[]{:S(2)}) collective-permute-start(bf16[1136,128]{1,0:T(8,128)(2,1)} %bitcast.17), channel_id=1, source_target_pairs={{0,192},{1,193},{2,194},{3,195},{4,196},{5,197},{6,198},{7,199},{8... | collective-permute-start | bytes 872456 | tf_op jit(solution)/shard_map/ppermute | solution.py:24
  35.0 5.0 %collective-permute-done.1 = bf16[1136,128]{1,0:T(8,128)(2,1)S(1)} collective-permute-done((bf16[1136,128]{1,0:T(8,128)(2,1)}, bf16[1136,128]{1,0:T(8,128)(2,1)S(1)}, u32[]{:S(2)}, u32[]{:S(2)}) %collective-permute-start.1) | collective-permute-done | bytes 290848 | tf_op jit(solution)/shard_map/ppermute | solution.py:24
  39.9 4.4 %collective-permute-done = bf16[1136,128]{1,0:T(8,128)(2,1)S(1)} collective-permute-done((bf16[1136,128]{1,0:T(8,128)(2,1)}, bf16[1136,128]{1,0:T(8,128)(2,1)S(1)}, u32[]{:S(2)}, u32[]{:S(2)}) %collective-permute-start) | collective-permute-done | bytes 290848 | tf_op jit(solution)/shard_map/ppermute | solution.py:24
  44.4 2.5 %collective-permute-start.7 = (bf16[1136,128]{1,0:T(8,128)(2,1)S(1)}, bf16[1136,128]{1,0:T(8,128)(2,1)S(1)}, u32[]{:S(2)}, u32[]{:S(2)}) collective-permute-start(bf16[1136,128]{1,0:T(8,128)(2,1)S(1)} %collective-permute-done.3), channel_id=1, source_target_pairs={{0,64},{1,65},{2,66},{3,67},{4,68},{5,69},{6,70},{7,71},{8,72},{9,... | collective-permute-start | bytes 872456 | tf_op jit(solution)/shard_map/ppermute | solution.py:24
  46.9 3.0 %collective-permute-start.6 = (bf16[1136,128]{1,0:T(8,128)(2,1)S(1)}, bf16[1136,128]{1,0:T(8,128)(2,1)S(1)}, u32[]{:S(2)}, u32[]{:S(2)}) collective-permute-start(bf16[1136,128]{1,0:T(8,128)(2,1)S(1)} %collective-permute-done.3), channel_id=1, source_target_pairs={{0,128},{1,129},{2,130},{3,131},{4,132},{5,133},{6,134},{7,135},{8... | collective-permute-start | bytes 872456 | tf_op jit(solution)/shard_map/ppermute | solution.py:24
  49.9 4.0 %collective-permute-start.5 = (bf16[1136,128]{1,0:T(8,128)(2,1)S(1)}, bf16[1136,128]{1,0:T(8,128)(2,1)S(1)}, u32[]{:S(2)}, u32[]{:S(2)}) collective-permute-start(bf16[1136,128]{1,0:T(8,128)(2,1)S(1)} %collective-permute-done.3), channel_id=1, source_target_pairs={{0,192},{1,193},{2,194},{3,195},{4,196},{5,197},{6,198},{7,199},{8... | collective-permute-start | bytes 872456 | tf_op jit(solution)/shard_map/ppermute | solution.py:24
  55.1 1.9 %collective-permute-start.4 = (bf16[4,1136,128]{2,1,0:T(8,128)(2,1)S(1)}, bf16[4,1136,128]{2,1,0:T(8,128)(2,1)S(1)}, u32[]{:S(2)}, u32[]{:S(2)}) collective-permute-start(bf16[4,1136,128]{2,1,0:T(8,128)(2,1)S(1)} %pad_maximum_fusion.s0), channel_id=1, source_target_pairs={{0,32},{1,33},{2,34},{3,35},{4,36},{5,37},{6,38},{7,39},{8,40},{9,... | collective-permute-start | bytes 3489800 | tf_op jit(solution)/shard_map/ppermute | solution.py:24
  57.0 4.2 %all-gather.2.cloned.1.call-done.all_ref = bf16[2048,768]{1,0:T(8,128)(2,1)} async-done(((bf16[512,768]{1,0:T(8,128)(2,1)}), bf16[2048,768]{1,0:T(8,128)(2,1)}) %all-gather.2.cloned.1.call-update) | async-done | bytes 3145744 | tf_op jit(solution)/shard_map/all_gather | solution.py:180
  63.1 2.0 %prep.1.grads_ref = bf16[4,768,512]{2,1,0:T(8,128)(2,1)S(1)} custom-call(s32[5]{0:T(128)S(1)} %stack.53.at_ref, bf16[2048,768]{1,0:T(8,128)(2,1)S(1)} %copy-done), custom_call_target="tpu_custom_call" | custom-call | tf_op jit(solution)/shard_map/prep/pallas_call | solution.py:190
  67.3 3.6 %own.1.start_ref = f32[768,1136]{1,0:T(8,128)S(1)} custom-call(s32[5]{0:T(128)S(1)} %stack.53.at_ref, bf16[4,1136,128]{2,1,0:T(8,128)(2,1)S(1)} %pad_maximum_fusion.s0, bf16[4,1136,128]{2,1,0:T(8,128)(2,1)S(1)} %collective-permute-done.4.t0, bf16[4,768,512]{2,1,0:T(8,128)(2,1)S(1)} %prep.1.grads_ref, f32[8,128]{1,0:T(8,128)S(1)} %fence.3.token), custom_call_target="tpu_custom_call" | custom-call | tf_op jit(solution)/shard_map/own/pallas_call | solution.py:199
  70.8 3.8 %rest.1 = (f32[96,1152]{1,0:T(8,128)S(1)}, f32[96,1152]{1,0:T(8,128)S(1)}, f32[96,1152]{1,0:T(8,128)S(1)}, f32[96,1152]{1,0:T(8,128)S(1)}, f32[192,1152]{1,0:T(8,128)S(1)}, /*index=5*/f32[192,1152]{1,0:T(8,128)S(1)}) custom-call(s32[5]{0:T(128)S(1)} %stack.53.at_ref, bf16[4,1136,128]{2,1,0:T(8,128)(2,1)S(1)} %pad_maximum_fusion.1.s1, ...), custom_call_target="tpu_custom_call" | custom-call | tf_op jit(solution)/shard_map/rest/pallas_call | solution.py:205
  74.7 7.0 %collective-permute-start.13 = (f16[96,1152]{1,0:T(8,128)(2,1)S(1)}, f16[96,1152]{1,0:T(8,128)(2,1)S(1)}, u32[]{:S(2)}, u32[]{:S(2)}) collective-permute-start(f16[96,1152]{1,0:T(8,128)(2,1)S(1)} %convert_element_type.54), channel_id=1, source_target_pairs={{0,1},{1,0},{2,3},{3,2},{4,5},{5,4},{6,7},{7,6},{8,9},{9,8},{10,11... | collective-permute-start | bytes 663560 | tf_op jit(solution)/shard_map/ppermute | solution.py:24
  81.8 1.9 %collective-permute-start.12 = (f16[96,1152]{1,0:T(8,128)(2,1)S(1)}, f16[96,1152]{1,0:T(8,128)(2,1)S(1)}, u32[]{:S(2)}, u32[]{:S(2)}) collective-permute-start(f16[96,1152]{1,0:T(8,128)(2,1)S(1)} %convert_element_type.52), channel_id=1, source_target_pairs={{0,1},{1,0},{2,3},{3,2},{4,5},{5,4},{6,7},{7,6},{8,9},{9,8},{10,11... | collective-permute-start | bytes 663560 | tf_op jit(solution)/shard_map/ppermute | solution.py:24
  83.7 3.9 %collective-permute-start.10 = (f16[96,1152]{1,0:T(8,128)(2,1)S(1)}, f16[96,1152]{1,0:T(8,128)(2,1)S(1)}, u32[]{:S(2)}, u32[]{:S(2)}) collective-permute-start(f16[96,1152]{1,0:T(8,128)(2,1)S(1)} %convert_element_type.48), channel_id=1, source_target_pairs={{0,1},{1,0},{2,3},{3,2},{4,5},{5,4},{6,7},{7,6},{8,9},{9,8},{10,11... | collective-permute-start | bytes 663560 | tf_op jit(solution)/shard_map/ppermute | solution.py:24
  88.2 1.9 %collective-permute-start.14 = (f16[96,1152]{1,0:T(8,128)(2,1)S(1)}, f16[96,1152]{1,0:T(8,128)(2,1)S(1)}, u32[]{:S(2)}, u32[]{:S(2)}) collective-permute-start(f16[96,1152]{1,0:T(8,128)(2,1)S(1)} %convert_element_type.56), channel_id=1, source_target_pairs={{0,2},{1,3},{2,0},{3,1},{4,6},{5,7},{6,4},{7,5},{8,10},{9,11},{10,... | collective-permute-start | bytes 663560 | tf_op jit(solution)/shard_map/ppermute | solution.py:24
  90.2 3.8 %collective-permute-start.9 = (f16[96,1152]{1,0:T(8,128)(2,1)S(1)}, f16[96,1152]{1,0:T(8,128)(2,1)S(1)}, u32[]{:S(2)}, u32[]{:S(2)}) collective-permute-start(f16[96,1152]{1,0:T(8,128)(2,1)S(1)} %convert_element_type.46), channel_id=1, source_target_pairs={{0,1},{1,0},{2,3},{3,2},{4,5},{5,4},{6,7},{7,6},{8,9},{9,8},{10,11... | collective-permute-start | bytes 663560 | tf_op jit(solution)/shard_map/ppermute | solution.py:24
  94.0 6.1 %collective-permute-done.10 = f16[96,1152]{1,0:T(8,128)(2,1)S(1)} collective-permute-done((f16[96,1152]{1,0:T(8,128)(2,1)S(1)}, f16[96,1152]{1,0:T(8,128)(2,1)S(1)}, u32[]{:S(2)}, u32[]{:S(2)}) %collective-permute-start.10) | collective-permute-done | bytes 221216 | tf_op jit(solution)/shard_map/ppermute | solution.py:24
  100.4 2.5 %collective-permute-start.11 = (f16[96,1152]{1,0:T(8,128)(2,1)S(1)}, f16[96,1152]{1,0:T(8,128)(2,1)S(1)}, u32[]{:S(2)}, u32[]{:S(2)}) collective-permute-start(f16[96,1152]{1,0:T(8,128)(2,1)S(1)} %convert_element_type.50), channel_id=1, source_target_pairs={{0,2},{1,3},{2,0},{3,1},{4,6},{5,7},{6,4},{7,5},{8,10},{9,11},{10,... | collective-permute-start | bytes 663560 | tf_op jit(solution)/shard_map/ppermute | solution.py:24
  103.2 7.0 %collective-permute-start.15 = (f16[96,1152]{1,0:T(8,128)(2,1)S(1)}, f16[96,1152]{1,0:T(8,128)(2,1)S(1)}, u32[]{:S(2)}, u32[]{:S(2)}) collective-permute-start(f16[96,1152]{1,0:T(8,128)(2,1)S(1)} %convert_element_type.58), channel_id=1, source_target_pairs={{0,4},{1,5},{2,6},{3,7},{4,0},{5,1},{6,2},{7,3},{8,12},{9,13},{10,... | collective-permute-start | bytes 663560 | tf_op jit(solution)/shard_map/ppermute | solution.py:24
  110.4 11.7 %collective-permute-done.11 = f16[96,1152]{1,0:T(8,128)(2,1)S(1)} collective-permute-done((f16[96,1152]{1,0:T(8,128)(2,1)S(1)}, f16[96,1152]{1,0:T(8,128)(2,1)S(1)}, u32[]{:S(2)}, u32[]{:S(2)}) %collective-permute-start.11) | collective-permute-done | bytes 221216 | tf_op jit(solution)/shard_map/ppermute | solution.py:24
  122.2 7.5 %collective-permute-done.15 = f16[96,1152]{1,0:T(8,128)(2,1)S(1)} collective-permute-done((f16[96,1152]{1,0:T(8,128)(2,1)S(1)}, f16[96,1152]{1,0:T(8,128)(2,1)S(1)}, u32[]{:S(2)}, u32[]{:S(2)}) %collective-permute-start.15) | collective-permute-done | bytes 221216 | tf_op jit(solution)/shard_map/ppermute | solution.py:24
  (44 shorter events, 9.8 us)
Async XLA Ops:
  6.5 54.7 %all-gather.2.cloned.1.call-start = ((), (), s32[]{:S(2)}) async-start(), calls=%async_computation | async-start | bytes 3932160 | tf_op jit(solution)/shard_map/all_gather | solution.py:180
  7.3 27.4 %collective-permute-start.3 = (bf16[1136,128]{1,0:T(8,128)(2,1)}, bf16[1136,128]{1,0:T(8,128)(2,1)S(1)}, u32[]{:S(2)}, u32[]{:S(2)}) collective-permute-start(bf16[1136,128]{1,0:T(8,128)(2,1)} %bitcast.14), channel_id=1, source_target_pairs={{0,256},{1,257},{2,258},{3,259},{4,260},{5,261},{6,262},{7,263},{8... | collective-permute-start | bytes 872456 | tf_op jit(solution)/shard_map/ppermute | solution.py:24
  23.0 12.0 %collective-permute-start.2 = (bf16[1136,128]{1,0:T(8,128)(2,1)}, bf16[1136,128]{1,0:T(8,128)(2,1)S(1)}, u32[]{:S(2)}, u32[]{:S(2)}) collective-permute-start(bf16[1136,128]{1,0:T(8,128)(2,1)} %bitcast.15), channel_id=1, source_target_pairs={{0,64},{1,65},{2,66},{3,67},{4,68},{5,69},{6,70},{7,71},{8,72},{9,... | collective-permute-start | bytes 872456 | tf_op jit(solution)/shard_map/ppermute | solution.py:24
  26.4 13.5 %collective-permute-start.1 = (bf16[1136,128]{1,0:T(8,128)(2,1)}, bf16[1136,128]{1,0:T(8,128)(2,1)S(1)}, u32[]{:S(2)}, u32[]{:S(2)}) collective-permute-start(bf16[1136,128]{1,0:T(8,128)(2,1)} %bitcast.16), channel_id=1, source_target_pairs={{0,128},{1,129},{2,130},{3,131},{4,132},{5,133},{6,134},{7,135},{8... | collective-permute-start | bytes 872456 | tf_op jit(solution)/shard_map/ppermute | solution.py:24
  29.5 14.9 %collective-permute-start = (bf16[1136,128]{1,0:T(8,128)(2,1)}, bf16[1136,128]{1,0:T(8,128)(2,1)S(1)}, u32[]{:S(2)}, u32[]{:S(2)}) collective-permute-start(bf16[1136,128]{1,0:T(8,128)(2,1)} %bitcast.17), channel_id=1, source_target_pairs={{0,192},{1,193},{2,194},{3,195},{4,196},{5,197},{6,198},{7,199},{8... | collective-permute-start | bytes 872456 | tf_op jit(solution)/shard_map/ppermute | solution.py:24
  44.4 20.8 %collective-permute-start.7 = (bf16[1136,128]{1,0:T(8,128)(2,1)S(1)}, bf16[1136,128]{1,0:T(8,128)(2,1)S(1)}, u32[]{:S(2)}, u32[]{:S(2)}) collective-permute-start(bf16[1136,128]{1,0:T(8,128)(2,1)S(1)} %collective-permute-done.3), channel_id=1, source_target_pairs={{0,64},{1,65},{2,66},{3,67},{4,68},{5,69},{6,70},{7,71},{8,72},{9,... | collective-permute-start | bytes 872456 | tf_op jit(solution)/shard_map/ppermute | solution.py:24
  46.9 18.3 %collective-permute-start.6 = (bf16[1136,128]{1,0:T(8,128)(2,1)S(1)}, bf16[1136,128]{1,0:T(8,128)(2,1)S(1)}, u32[]{:S(2)}, u32[]{:S(2)}) collective-permute-start(bf16[1136,128]{1,0:T(8,128)(2,1)S(1)} %collective-permute-done.3), channel_id=1, source_target_pairs={{0,128},{1,129},{2,130},{3,131},{4,132},{5,133},{6,134},{7,135},{8... | collective-permute-start | bytes 872456 | tf_op jit(solution)/shard_map/ppermute | solution.py:24
  49.9 15.3 %collective-permute-start.5 = (bf16[1136,128]{1,0:T(8,128)(2,1)S(1)}, bf16[1136,128]{1,0:T(8,128)(2,1)S(1)}, u32[]{:S(2)}, u32[]{:S(2)}) collective-permute-start(bf16[1136,128]{1,0:T(8,128)(2,1)S(1)} %collective-permute-done.3), channel_id=1, source_target_pairs={{0,192},{1,193},{2,194},{3,195},{4,196},{5,197},{6,198},{7,199},{8... | collective-permute-start | bytes 872456 | tf_op jit(solution)/shard_map/ppermute | solution.py:24
  55.1 12.2 %collective-permute-start.4 = (bf16[4,1136,128]{2,1,0:T(8,128)(2,1)S(1)}, bf16[4,1136,128]{2,1,0:T(8,128)(2,1)S(1)}, u32[]{:S(2)}, u32[]{:S(2)}) collective-permute-start(bf16[4,1136,128]{2,1,0:T(8,128)(2,1)S(1)} %pad_maximum_fusion.s0), channel_id=1, source_target_pairs={{0,32},{1,33},{2,34},{3,35},{4,36},{5,37},{6,38},{7,39},{8,40},{9,... | collective-permute-start | bytes 3489800 | tf_op jit(solution)/shard_map/ppermute | solution.py:24
  61.2 1.9 %copy-start = (bf16[2048,768]{1,0:T(8,128)(2,1)S(1)}, bf16[2048,768]{1,0:T(8,128)(2,1)}, u32[]{:S(2)}) copy-start(bf16[2048,768]{1,0:T(8,128)(2,1)} %all-gather.2.cloned.1.call-done.all_ref) | copy-start | bytes 9437188
  65.3 5.5 %collective-permute-start.8 = (bf16[4,1136,128]{2,1,0:T(8,128)(2,1)S(1)}, bf16[4,1136,128]{2,1,0:T(8,128)(2,1)S(1)}, u32[]{:S(2)}, u32[]{:S(2)}) collective-permute-start(bf16[4,1136,128]{2,1,0:T(8,128)(2,1)S(1)} %pad_maximum_fusion.1.s1), channel_id=1, source_target_pairs={{0,32},{1,33},{2,34},{3,35},{4,36},{5,37},{6,38},{7,39},{8,40},{9,... | collective-permute-start | bytes 3489800 | tf_op jit(solution)/shard_map/ppermute | solution.py:24
  74.7 13.3 %collective-permute-start.13 = (f16[96,1152]{1,0:T(8,128)(2,1)S(1)}, f16[96,1152]{1,0:T(8,128)(2,1)S(1)}, u32[]{:S(2)}, u32[]{:S(2)}) collective-permute-start(f16[96,1152]{1,0:T(8,128)(2,1)S(1)} %convert_element_type.54), channel_id=1, source_target_pairs={{0,1},{1,0},{2,3},{3,2},{4,5},{5,4},{6,7},{7,6},{8,9},{9,8},{10,11... | collective-permute-start | bytes 663560 | tf_op jit(solution)/shard_map/ppermute | solution.py:24
  81.8 21.1 %collective-permute-start.12 = (f16[96,1152]{1,0:T(8,128)(2,1)S(1)}, f16[96,1152]{1,0:T(8,128)(2,1)S(1)}, u32[]{:S(2)}, u32[]{:S(2)}) collective-permute-start(f16[96,1152]{1,0:T(8,128)(2,1)S(1)} %convert_element_type.52), channel_id=1, source_target_pairs={{0,1},{1,0},{2,3},{3,2},{4,5},{5,4},{6,7},{7,6},{8,9},{9,8},{10,11... | collective-permute-start | bytes 663560 | tf_op jit(solution)/shard_map/ppermute | solution.py:24
  83.7 16.5 %collective-permute-start.10 = (f16[96,1152]{1,0:T(8,128)(2,1)S(1)}, f16[96,1152]{1,0:T(8,128)(2,1)S(1)}, u32[]{:S(2)}, u32[]{:S(2)}) collective-permute-start(f16[96,1152]{1,0:T(8,128)(2,1)S(1)} %convert_element_type.48), channel_id=1, source_target_pairs={{0,1},{1,0},{2,3},{3,2},{4,5},{5,4},{6,7},{7,6},{8,9},{9,8},{10,11... | collective-permute-start | bytes 663560 | tf_op jit(solution)/shard_map/ppermute | solution.py:24
  88.2 14.8 %collective-permute-start.14 = (f16[96,1152]{1,0:T(8,128)(2,1)S(1)}, f16[96,1152]{1,0:T(8,128)(2,1)S(1)}, u32[]{:S(2)}, u32[]{:S(2)}) collective-permute-start(f16[96,1152]{1,0:T(8,128)(2,1)S(1)} %convert_element_type.56), channel_id=1, source_target_pairs={{0,2},{1,3},{2,0},{3,1},{4,6},{5,7},{6,4},{7,5},{8,10},{9,11},{10,... | collective-permute-start | bytes 663560 | tf_op jit(solution)/shard_map/ppermute | solution.py:24
  90.2 20.1 %collective-permute-start.9 = (f16[96,1152]{1,0:T(8,128)(2,1)S(1)}, f16[96,1152]{1,0:T(8,128)(2,1)S(1)}, u32[]{:S(2)}, u32[]{:S(2)}) collective-permute-start(f16[96,1152]{1,0:T(8,128)(2,1)S(1)} %convert_element_type.46), channel_id=1, source_target_pairs={{0,1},{1,0},{2,3},{3,2},{4,5},{5,4},{6,7},{7,6},{8,9},{9,8},{10,11... | collective-permute-start | bytes 663560 | tf_op jit(solution)/shard_map/ppermute | solution.py:24
  100.4 21.7 %collective-permute-start.11 = (f16[96,1152]{1,0:T(8,128)(2,1)S(1)}, f16[96,1152]{1,0:T(8,128)(2,1)S(1)}, u32[]{:S(2)}, u32[]{:S(2)}) collective-permute-start(f16[96,1152]{1,0:T(8,128)(2,1)S(1)} %convert_element_type.50), channel_id=1, source_target_pairs={{0,2},{1,3},{2,0},{3,1},{4,6},{5,7},{6,4},{7,5},{8,10},{9,11},{10,... | collective-permute-start | bytes 663560 | tf_op jit(solution)/shard_map/ppermute | solution.py:24
  103.2 26.5 %collective-permute-start.15 = (f16[96,1152]{1,0:T(8,128)(2,1)S(1)}, f16[96,1152]{1,0:T(8,128)(2,1)S(1)}, u32[]{:S(2)}, u32[]{:S(2)}) collective-permute-start(f16[96,1152]{1,0:T(8,128)(2,1)S(1)} %convert_element_type.58), channel_id=1, source_target_pairs={{0,4},{1,5},{2,6},{3,7},{4,0},{5,1},{6,2},{7,3},{8,12},{9,13},{10,... | collective-permute-start | bytes 663560 | tf_op jit(solution)/shard_map/ppermute | solution.py:24
Sparse Core Ops, SparseCore 0:
  9.5 51.6 all-gather.1

commit v4 on v3

--- a/solution.py
+++ b/solution.py
@@ -115,40 +115,47 @@
             lax.dot_general(grads_ref[j], acts_ref[lo:hi, j * 512:(j + 1) * 512], NT, preferred_element_type=f32) for j in range(2))
 
 
+def coded(total, size):
+    total = total * jnp.exp2(7 - size)
+    return total * jnp.abs(total)
+
+
+def decoded(message, size):
+    root = jnp.sqrt(jnp.abs(message)) * jnp.exp2(size - 7)
+    return jnp.where(message < 0, -root, root)
+
+
 def rest_kernel(at_ref, s1, t1, grads_ref, start_ref, *refs):
     far0_ref, far1_ref, near0_ref, near1_ref, keep_far_ref, keep_near_ref, acts_ref, sems = refs
     for copy in spread(at_ref, s1, t1, acts_ref, sems):
         copy.wait()
-    sends = (far0_ref, far1_ref, near0_ref, near1_ref)
-    top = None
+    places = ((far0_ref, 0), (far1_ref, 96), (keep_far_ref, 192), (near0_ref, 384), (near1_ref, 480), (keep_near_ref, 576))
+    tops = []
     for lo, hi in TILES:
         part = start_ref[:, lo:hi] + sum(
             lax.dot_general(grads_ref[2 + j], acts_ref[lo:hi, j * 512:(j + 1) * 512], NT, preferred_element_type=f32) for j in range(2))
-        for ref, first in zip(sends, (0, 96, 384, 480)):
-            ref[:, lo:hi] = part[first:first + 96]
-        keep_far_ref[:, lo:hi] = part[192:384]
-        keep_near_ref[:, lo:hi] = part[576:]
-        part = jnp.max(jnp.abs(part), axis=0, keepdims=True)
-        part = jnp.max(part, axis=1, keepdims=True)
-        top = part if top is None else jnp.maximum(top, part)
-    size = jnp.clip(jnp.ceil(jnp.log2(top)) + 1, -100, 100)
-    scale = jnp.exp2(15 - size)
-    for ref in sends:
-        ref[:, :1136] = ref[:, :1136] * scale
-    for ref in (*sends, keep_far_ref, keep_near_ref):
-        ref[:, 1136:] = jnp.broadcast_to(size, (ref.shape[0], 16))
+        for ref, first in places:
+            ref[:, lo:hi] = part[first:first + ref.shape[0]]
+        tops.append(jnp.max(jnp.abs(part), axis=1, keepdims=True))
+    size = jnp.clip(jnp.ceil(jnp.log2(functools.reduce(jnp.maximum, tops))) + 1, -100, 100)
+    for ref, first in places:
+        rows = ref.shape[0]
+        its = size[first:first + rows]
+        ref[:, 1136:] = jnp.broadcast_to(its, (rows, 16))
+        if rows == 96:
+            ref[:, :1136] = coded(ref[:, :1136], its)
 
 
 def stage_kernel(spans, keep_ref, message_ref, *out_refs):
     message = message_ref[...]
     size = message[:, 1136:1137]
-    total = keep_ref[...] + message * jnp.exp2(size - 15)
+    total = keep_ref[...] + decoded(message, size)
     size = jnp.maximum(keep_ref[:, 1136:1137], size) + 1
     lane = lax.broadcasted_iota(jnp.int32, total.shape, 1)
     kept = jnp.where(lane < 1136, total, size)
-    sent = jnp.where(lane < 1136, total * jnp.exp2(15 - size), size)
-    for (first, rows, scaled), ref in zip(spans, out_refs):
-        ref[...] = (sent if scaled else kept)[first:first + rows]
+    sent = jnp.where(lane < 1136, coded(total, size), size)
+    for (first, rows, on), ref in zip(spans, out_refs):
+        ref[...] = (sent if on else kept)[first:first + rows]
 
 
 def stage(keep, message, *spans):
@@ -160,16 +167,13 @@
 
 def final_kernel(near_ref, message_ref, out_ref):
     message = message_ref[...]
-    out_ref[...] = (near_ref[...] + message * jnp.exp2(message[:, 1136:1137] - 15))[:, :1136]
+    out_ref[...] = (near_ref[...] + decoded(message, message[:, 1136:1137]))[:, :1136]
 
 
 def again(token):
     return pl.pallas_call(
         fence_kernel, out_shape=shape((8, 128), f32), in_specs=[VM], out_specs=VM, compiler_params=PARAMS, name="fence",
     )(token)
-
-
-FIRST = 64
 
 
 def body(activations, out_grads):

time: 138 us -> 139 us (level)
  no operation moved by 1% of the time
where the time goes in v4:
time: 139 us; the launch traced here: 138 us
  starting transfers between devices  67.7 us (49%)
  waiting for transfers between devices  40.7 us (29%)
  between operations  13.8 us (10%)
  Pallas kernels  12 us (9%)
  local copies, waits for them, and re-layouts  2.1 us (2%)
  other arithmetic  1.67 us (1%)
    ppermute x16, starting transfers between devices, permute(): return lax.ppermute(value, AXES, pairs)  67.7 us
    ppermute x16, waiting for transfers between devices, permute(): return lax.ppermute(value, AXES, pairs)  35.9 us
    all_gather x1, waiting for transfers between devices, body(): every_grad = lax.all_gather(out_grads, 'col', axis=0, tiled=True)  4.17 us
    pallas_call x1, Pallas kernels, body(): pl.pallas_call(rest_kernel, out_shape=(shape((96, 1152), f32),) * 4 + (sh...  3.94 us
    pallas_call x1, Pallas kernels, body(): pl.pallas_call(own_kernel, out_shape=shape((768, 1136), f32), in_specs=[S...  3.55 us
  transfers between devices with their start and end apart: 17, of which 9 were waited for; matrix products, arithmetic and copies ran while one was open for 1% of the time, Pallas kernels for 5%

profile of v4, /device:TPU:2, one launch (start us, length us, event | category | flops | bytes accessed | tf_op | source)
XLA Modules:
  0.0 138.0 jit_solution(11057665274311135009)
XLA Ops:
  7.3 15.7 %collective-permute-start.3 = (bf16[1136,128]{1,0:T(8,128)(2,1)}, bf16[1136,128]{1,0:T(8,128)(2,1)S(1)}, u32[]{:S(2)}, u32[]{:S(2)}) collective-permute-start(bf16[1136,128]{1,0:T(8,128)(2,1)} %bitcast.14), channel_id=1, source_target_pairs={{0,256},{1,257},{2,258},{3,259},{4,260},{5,261},{6,262},{7,263},{8... | collective-permute-start | bytes 872456 | tf_op jit(solution)/shard_map/ppermute | solution.py:24
  23.0 3.4 %collective-permute-start.2 = (bf16[1136,128]{1,0:T(8,128)(2,1)}, bf16[1136,128]{1,0:T(8,128)(2,1)S(1)}, u32[]{:S(2)}, u32[]{:S(2)}) collective-permute-start(bf16[1136,128]{1,0:T(8,128)(2,1)} %bitcast.15), channel_id=1, source_target_pairs={{0,64},{1,65},{2,66},{3,67},{4,68},{5,69},{6,70},{7,71},{8,72},{9,... | collective-permute-start | bytes 872456 | tf_op jit(solution)/shard_map/ppermute | solution.py:24
  26.4 3.0 %collective-permute-start.1 = (bf16[1136,128]{1,0:T(8,128)(2,1)}, bf16[1136,128]{1,0:T(8,128)(2,1)S(1)}, u32[]{:S(2)}, u32[]{:S(2)}) collective-permute-start(bf16[1136,128]{1,0:T(8,128)(2,1)} %bitcast.16), channel_id=1, source_target_pairs={{0,128},{1,129},{2,130},{3,131},{4,132},{5,133},{6,134},{7,135},{8... | collective-permute-start | bytes 872456 | tf_op jit(solution)/shard_map/ppermute | solution.py:24
  29.5 4.1 %collective-permute-start = (bf16[1136,128]{1,0:T(8,128)(2,1)}, bf16[1136,128]{1,0:T(8,128)(2,1)S(1)}, u32[]{:S(2)}, u32[]{:S(2)}) collective-permute-start(bf16[1136,128]{1,0:T(8,128)(2,1)} %bitcast.17), channel_id=1, source_target_pairs={{0,192},{1,193},{2,194},{3,195},{4,196},{5,197},{6,198},{7,199},{8... | collective-permute-start | bytes 872456 | tf_op jit(solution)/shard_map/ppermute | solution.py:24
  35.0 5.0 %collective-permute-done.1 = bf16[1136,128]{1,0:T(8,128)(2,1)S(1)} collective-permute-done((bf16[1136,128]{1,0:T(8,128)(2,1)}, bf16[1136,128]{1,0:T(8,128)(2,1)S(1)}, u32[]{:S(2)}, u32[]{:S(2)}) %collective-permute-start.1) | collective-permute-done | bytes 290848 | tf_op jit(solution)/shard_map/ppermute | solution.py:24
  39.9 4.4 %collective-permute-done = bf16[1136,128]{1,0:T(8,128)(2,1)S(1)} collective-permute-done((bf16[1136,128]{1,0:T(8,128)(2,1)}, bf16[1136,128]{1,0:T(8,128)(2,1)S(1)}, u32[]{:S(2)}, u32[]{:S(2)}) %collective-permute-start) | collective-permute-done | bytes 290848 | tf_op jit(solution)/shard_map/ppermute | solution.py:24
  44.4 2.5 %collective-permute-start.7 = (bf16[1136,128]{1,0:T(8,128)(2,1)S(1)}, bf16[1136,128]{1,0:T(8,128)(2,1)S(1)}, u32[]{:S(2)}, u32[]{:S(2)}) collective-permute-start(bf16[1136,128]{1,0:T(8,128)(2,1)S(1)} %collective-permute-done.3), channel_id=1, source_target_pairs={{0,64},{1,65},{2,66},{3,67},{4,68},{5,69},{6,70},{7,71},{8,72},{9,... | collective-permute-start | bytes 872456 | tf_op jit(solution)/shard_map/ppermute | solution.py:24
  46.9 3.0 %collective-permute-start.6 = (bf16[1136,128]{1,0:T(8,128)(2,1)S(1)}, bf16[1136,128]{1,0:T(8,128)(2,1)S(1)}, u32[]{:S(2)}, u32[]{:S(2)}) collective-permute-start(bf16[1136,128]{1,0:T(8,128)(2,1)S(1)} %collective-permute-done.3), channel_id=1, source_target_pairs={{0,128},{1,129},{2,130},{3,131},{4,132},{5,133},{6,134},{7,135},{8... | collective-permute-start | bytes 872456 | tf_op jit(solution)/shard_map/ppermute | solution.py:24
  49.9 4.0 %collective-permute-start.5 = (bf16[1136,128]{1,0:T(8,128)(2,1)S(1)}, bf16[1136,128]{1,0:T(8,128)(2,1)S(1)}, u32[]{:S(2)}, u32[]{:S(2)}) collective-permute-start(bf16[1136,128]{1,0:T(8,128)(2,1)S(1)} %collective-permute-done.3), channel_id=1, source_target_pairs={{0,192},{1,193},{2,194},{3,195},{4,196},{5,197},{6,198},{7,199},{8... | collective-permute-start | bytes 872456 | tf_op jit(solution)/shard_map/ppermute | solution.py:24
  55.1 1.9 %collective-permute-start.4 = (bf16[4,1136,128]{2,1,0:T(8,128)(2,1)S(1)}, bf16[4,1136,128]{2,1,0:T(8,128)(2,1)S(1)}, u32[]{:S(2)}, u32[]{:S(2)}) collective-permute-start(bf16[4,1136,128]{2,1,0:T(8,128)(2,1)S(1)} %pad_maximum_fusion.s0), channel_id=1, source_target_pairs={{0,32},{1,33},{2,34},{3,35},{4,36},{5,37},{6,38},{7,39},{8,40},{9,... | collective-permute-start | bytes 3489800 | tf_op jit(solution)/shard_map/ppermute | solution.py:24
  57.0 4.2 %all-gather.2.cloned.1.call-done.all_ref = bf16[2048,768]{1,0:T(8,128)(2,1)} async-done(((bf16[512,768]{1,0:T(8,128)(2,1)}), bf16[2048,768]{1,0:T(8,128)(2,1)}) %all-gather.2.cloned.1.call-update) | async-done | bytes 3145744 | tf_op jit(solution)/shard_map/all_gather | solution.py:184
  63.1 2.0 %prep.1.grads_ref = bf16[4,768,512]{2,1,0:T(8,128)(2,1)S(1)} custom-call(s32[5]{0:T(128)S(1)} %stack.53.at_ref, bf16[2048,768]{1,0:T(8,128)(2,1)S(1)} %copy-done), custom_call_target="tpu_custom_call" | custom-call | tf_op jit(solution)/shard_map/prep/pallas_call | solution.py:194
  65.3 1.9 %collective-permute-start.8 = (bf16[4,1136,128]{2,1,0:T(8,128)(2,1)S(1)}, bf16[4,1136,128]{2,1,0:T(8,128)(2,1)S(1)}, u32[]{:S(2)}, u32[]{:S(2)}) collective-permute-start(bf16[4,1136,128]{2,1,0:T(8,128)(2,1)S(1)} %pad_maximum_fusion.1.s1), channel_id=1, source_target_pairs={{0,32},{1,33},{2,34},{3,35},{4,36},{5,37},{6,38},{7,39},{8,40},{9,... | collective-permute-start | bytes 3489800 | tf_op jit(solution)/shard_map/ppermute | solution.py:24
  67.3 3.6 %own.1.start_ref = f32[768,1136]{1,0:T(8,128)S(1)} custom-call(s32[5]{0:T(128)S(1)} %stack.53.at_ref, bf16[4,1136,128]{2,1,0:T(8,128)(2,1)S(1)} %pad_maximum_fusion.s0, bf16[4,1136,128]{2,1,0:T(8,128)(2,1)S(1)} %collective-permute-done.4.t0, bf16[4,768,512]{2,1,0:T(8,128)(2,1)S(1)} %prep.1.grads_ref, f32[8,128]{1,0:T(8,128)S(1)} %fence.3.token), custom_call_target="tpu_custom_call" | custom-call | tf_op jit(solution)/shard_map/own/pallas_call | solution.py:203
  70.8 3.9 %rest.1 = (f32[96,1152]{1,0:T(8,128)S(1)}, f32[96,1152]{1,0:T(8,128)S(1)}, f32[96,1152]{1,0:T(8,128)S(1)}, f32[96,1152]{1,0:T(8,128)S(1)}, f32[192,1152]{1,0:T(8,128)S(1)}, /*index=5*/f32[192,1152]{1,0:T(8,128)S(1)}) custom-call(s32[5]{0:T(128)S(1)} %stack.53.at_ref, bf16[4,1136,128]{2,1,0:T(8,128)(2,1)S(1)} %pad_maximum_fusion.1.s1, ...), custom_call_target="tpu_custom_call" | custom-call | tf_op jit(solution)/shard_map/rest/pallas_call | solution.py:209
  74.9 7.0 %collective-permute-start.13 = (f16[96,1152]{1,0:T(8,128)(2,1)S(1)}, f16[96,1152]{1,0:T(8,128)(2,1)S(1)}, u32[]{:S(2)}, u32[]{:S(2)}) collective-permute-start(f16[96,1152]{1,0:T(8,128)(2,1)S(1)} %convert_element_type.54), channel_id=1, source_target_pairs={{0,1},{1,0},{2,3},{3,2},{4,5},{5,4},{6,7},{7,6},{8,9},{9,8},{10,11... | collective-permute-start | bytes 663560 | tf_op jit(solution)/shard_map/ppermute | solution.py:24
  81.9 1.9 %collective-permute-start.12 = (f16[96,1152]{1,0:T(8,128)(2,1)S(1)}, f16[96,1152]{1,0:T(8,128)(2,1)S(1)}, u32[]{:S(2)}, u32[]{:S(2)}) collective-permute-start(f16[96,1152]{1,0:T(8,128)(2,1)S(1)} %convert_element_type.52), channel_id=1, source_target_pairs={{0,1},{1,0},{2,3},{3,2},{4,5},{5,4},{6,7},{7,6},{8,9},{9,8},{10,11... | collective-permute-start | bytes 663560 | tf_op jit(solution)/shard_map/ppermute | solution.py:24
  83.8 3.9 %collective-permute-start.10 = (f16[96,1152]{1,0:T(8,128)(2,1)S(1)}, f16[96,1152]{1,0:T(8,128)(2,1)S(1)}, u32[]{:S(2)}, u32[]{:S(2)}) collective-permute-start(f16[96,1152]{1,0:T(8,128)(2,1)S(1)} %convert_element_type.48), channel_id=1, source_target_pairs={{0,1},{1,0},{2,3},{3,2},{4,5},{5,4},{6,7},{7,6},{8,9},{9,8},{10,11... | collective-permute-start | bytes 663560 | tf_op jit(solution)/shard_map/ppermute | solution.py:24
  90.5 3.8 %collective-permute-start.9 = (f16[96,1152]{1,0:T(8,128)(2,1)S(1)}, f16[96,1152]{1,0:T(8,128)(2,1)S(1)}, u32[]{:S(2)}, u32[]{:S(2)}) collective-permute-start(f16[96,1152]{1,0:T(8,128)(2,1)S(1)} %convert_element_type.46), channel_id=1, source_target_pairs={{0,1},{1,0},{2,3},{3,2},{4,5},{5,4},{6,7},{7,6},{8,9},{9,8},{10,11... | collective-permute-start | bytes 663560 | tf_op jit(solution)/shard_map/ppermute | solution.py:24
  94.3 5.9 %collective-permute-done.10 = f16[96,1152]{1,0:T(8,128)(2,1)S(1)} collective-permute-done((f16[96,1152]{1,0:T(8,128)(2,1)S(1)}, f16[96,1152]{1,0:T(8,128)(2,1)S(1)}, u32[]{:S(2)}, u32[]{:S(2)}) %collective-permute-start.10) | collective-permute-done | bytes 221216 | tf_op jit(solution)/shard_map/ppermute | solution.py:24
  100.5 2.6 %collective-permute-start.11 = (f16[96,1152]{1,0:T(8,128)(2,1)S(1)}, f16[96,1152]{1,0:T(8,128)(2,1)S(1)}, u32[]{:S(2)}, u32[]{:S(2)}) collective-permute-start(f16[96,1152]{1,0:T(8,128)(2,1)S(1)} %convert_element_type.50), channel_id=1, source_target_pairs={{0,2},{1,3},{2,0},{3,1},{4,6},{5,7},{6,4},{7,5},{8,10},{9,11},{10,... | collective-permute-start | bytes 663560 | tf_op jit(solution)/shard_map/ppermute | solution.py:24
  103.7 7.0 %collective-permute-start.15 = (f16[96,1152]{1,0:T(8,128)(2,1)S(1)}, f16[96,1152]{1,0:T(8,128)(2,1)S(1)}, u32[]{:S(2)}, u32[]{:S(2)}) collective-permute-start(f16[96,1152]{1,0:T(8,128)(2,1)S(1)} %convert_element_type.58), channel_id=1, source_target_pairs={{0,4},{1,5},{2,6},{3,7},{4,0},{5,1},{6,2},{7,3},{8,12},{9,13},{10,... | collective-permute-start | bytes 663560 | tf_op jit(solution)/shard_map/ppermute | solution.py:24
  111.0 11.1 %collective-permute-done.11 = f16[96,1152]{1,0:T(8,128)(2,1)S(1)} collective-permute-done((f16[96,1152]{1,0:T(8,128)(2,1)S(1)}, f16[96,1152]{1,0:T(8,128)(2,1)S(1)}, u32[]{:S(2)}, u32[]{:S(2)}) %collective-permute-start.11) | collective-permute-done | bytes 221216 | tf_op jit(solution)/shard_map/ppermute | solution.py:24
  122.4 7.8 %collective-permute-done.15 = f16[96,1152]{1,0:T(8,128)(2,1)S(1)} collective-permute-done((f16[96,1152]{1,0:T(8,128)(2,1)S(1)}, f16[96,1152]{1,0:T(8,128)(2,1)S(1)}, u32[]{:S(2)}, u32[]{:S(2)}) %collective-permute-start.15) | collective-permute-done | bytes 221216 | tf_op jit(solution)/shard_map/ppermute | solution.py:24
  (44 shorter events, 10.6 us)
Async XLA Ops:
  6.5 54.7 %all-gather.2.cloned.1.call-start = ((), (), s32[]{:S(2)}) async-start(), calls=%async_computation | async-start | bytes 3932160 | tf_op jit(solution)/shard_map/all_gather | solution.py:184
  7.3 27.4 %collective-permute-start.3 = (bf16[1136,128]{1,0:T(8,128)(2,1)}, bf16[1136,128]{1,0:T(8,128)(2,1)S(1)}, u32[]{:S(2)}, u32[]{:S(2)}) collective-permute-start(bf16[1136,128]{1,0:T(8,128)(2,1)} %bitcast.14), channel_id=1, source_target_pairs={{0,256},{1,257},{2,258},{3,259},{4,260},{5,261},{6,262},{7,263},{8... | collective-permute-start | bytes 872456 | tf_op jit(solution)/shard_map/ppermute | solution.py:24
  23.0 12.0 %collective-permute-start.2 = (bf16[1136,128]{1,0:T(8,128)(2,1)}, bf16[1136,128]{1,0:T(8,128)(2,1)S(1)}, u32[]{:S(2)}, u32[]{:S(2)}) collective-permute-start(bf16[1136,128]{1,0:T(8,128)(2,1)} %bitcast.15), channel_id=1, source_target_pairs={{0,64},{1,65},{2,66},{3,67},{4,68},{5,69},{6,70},{7,71},{8,72},{9,... | collective-permute-start | bytes 872456 | tf_op jit(solution)/shard_map/ppermute | solution.py:24
  26.4 13.5 %collective-permute-start.1 = (bf16[1136,128]{1,0:T(8,128)(2,1)}, bf16[1136,128]{1,0:T(8,128)(2,1)S(1)}, u32[]{:S(2)}, u32[]{:S(2)}) collective-permute-start(bf16[1136,128]{1,0:T(8,128)(2,1)} %bitcast.16), channel_id=1, source_target_pairs={{0,128},{1,129},{2,130},{3,131},{4,132},{5,133},{6,134},{7,135},{8... | collective-permute-start | bytes 872456 | tf_op jit(solution)/shard_map/ppermute | solution.py:24
  29.5 14.9 %collective-permute-start = (bf16[1136,128]{1,0:T(8,128)(2,1)}, bf16[1136,128]{1,0:T(8,128)(2,1)S(1)}, u32[]{:S(2)}, u32[]{:S(2)}) collective-permute-start(bf16[1136,128]{1,0:T(8,128)(2,1)} %bitcast.17), channel_id=1, source_target_pairs={{0,192},{1,193},{2,194},{3,195},{4,196},{5,197},{6,198},{7,199},{8... | collective-permute-start | bytes 872456 | tf_op jit(solution)/shard_map/ppermute | solution.py:24
  44.4 20.8 %collective-permute-start.7 = (bf16[1136,128]{1,0:T(8,128)(2,1)S(1)}, bf16[1136,128]{1,0:T(8,128)(2,1)S(1)}, u32[]{:S(2)}, u32[]{:S(2)}) collective-permute-start(bf16[1136,128]{1,0:T(8,128)(2,1)S(1)} %collective-permute-done.3), channel_id=1, source_target_pairs={{0,64},{1,65},{2,66},{3,67},{4,68},{5,69},{6,70},{7,71},{8,72},{9,... | collective-permute-start | bytes 872456 | tf_op jit(solution)/shard_map/ppermute | solution.py:24
  46.9 18.3 %collective-permute-start.6 = (bf16[1136,128]{1,0:T(8,128)(2,1)S(1)}, bf16[1136,128]{1,0:T(8,128)(2,1)S(1)}, u32[]{:S(2)}, u32[]{:S(2)}) collective-permute-start(bf16[1136,128]{1,0:T(8,128)(2,1)S(1)} %collective-permute-done.3), channel_id=1, source_target_pairs={{0,128},{1,129},{2,130},{3,131},{4,132},{5,133},{6,134},{7,135},{8... | collective-permute-start | bytes 872456 | tf_op jit(solution)/shard_map/ppermute | solution.py:24
  49.9 15.3 %collective-permute-start.5 = (bf16[1136,128]{1,0:T(8,128)(2,1)S(1)}, bf16[1136,128]{1,0:T(8,128)(2,1)S(1)}, u32[]{:S(2)}, u32[]{:S(2)}) collective-permute-start(bf16[1136,128]{1,0:T(8,128)(2,1)S(1)} %collective-permute-done.3), channel_id=1, source_target_pairs={{0,192},{1,193},{2,194},{3,195},{4,196},{5,197},{6,198},{7,199},{8... | collective-permute-start | bytes 872456 | tf_op jit(solution)/shard_map/ppermute | solution.py:24
  55.1 12.2 %collective-permute-start.4 = (bf16[4,1136,128]{2,1,0:T(8,128)(2,1)S(1)}, bf16[4,1136,128]{2,1,0:T(8,128)(2,1)S(1)}, u32[]{:S(2)}, u32[]{:S(2)}) collective-permute-start(bf16[4,1136,128]{2,1,0:T(8,128)(2,1)S(1)} %pad_maximum_fusion.s0), channel_id=1, source_target_pairs={{0,32},{1,33},{2,34},{3,35},{4,36},{5,37},{6,38},{7,39},{8,40},{9,... | collective-permute-start | bytes 3489800 | tf_op jit(solution)/shard_map/ppermute | solution.py:24
  61.2 1.9 %copy-start = (bf16[2048,768]{1,0:T(8,128)(2,1)S(1)}, bf16[2048,768]{1,0:T(8,128)(2,1)}, u32[]{:S(2)}) copy-start(bf16[2048,768]{1,0:T(8,128)(2,1)} %all-gather.2.cloned.1.call-done.all_ref) | copy-start | bytes 9437188
  65.3 5.5 %collective-permute-start.8 = (bf16[4,1136,128]{2,1,0:T(8,128)(2,1)S(1)}, bf16[4,1136,128]{2,1,0:T(8,128)(2,1)S(1)}, u32[]{:S(2)}, u32[]{:S(2)}) collective-permute-start(bf16[4,1136,128]{2,1,0:T(8,128)(2,1)S(1)} %pad_maximum_fusion.1.s1), channel_id=1, source_target_pairs={{0,32},{1,33},{2,34},{3,35},{4,36},{5,37},{6,38},{7,39},{8,40},{9,... | collective-permute-start | bytes 3489800 | tf_op jit(solution)/shard_map/ppermute | solution.py:24
  74.9 13.3 %collective-permute-start.13 = (f16[96,1152]{1,0:T(8,128)(2,1)S(1)}, f16[96,1152]{1,0:T(8,128)(2,1)S(1)}, u32[]{:S(2)}, u32[]{:S(2)}) collective-permute-start(f16[96,1152]{1,0:T(8,128)(2,1)S(1)} %convert_element_type.54), channel_id=1, source_target_pairs={{0,1},{1,0},{2,3},{3,2},{4,5},{5,4},{6,7},{7,6},{8,9},{9,8},{10,11... | collective-permute-start | bytes 663560 | tf_op jit(solution)/shard_map/ppermute | solution.py:24
  81.9 21.2 %collective-permute-start.12 = (f16[96,1152]{1,0:T(8,128)(2,1)S(1)}, f16[96,1152]{1,0:T(8,128)(2,1)S(1)}, u32[]{:S(2)}, u32[]{:S(2)}) collective-permute-start(f16[96,1152]{1,0:T(8,128)(2,1)S(1)} %convert_element_type.52), channel_id=1, source_target_pairs={{0,1},{1,0},{2,3},{3,2},{4,5},{5,4},{6,7},{7,6},{8,9},{9,8},{10,11... | collective-permute-start | bytes 663560 | tf_op jit(solution)/shard_map/ppermute | solution.py:24
  83.8 16.4 %collective-permute-start.10 = (f16[96,1152]{1,0:T(8,128)(2,1)S(1)}, f16[96,1152]{1,0:T(8,128)(2,1)S(1)}, u32[]{:S(2)}, u32[]{:S(2)}) collective-permute-start(f16[96,1152]{1,0:T(8,128)(2,1)S(1)} %convert_element_type.48), channel_id=1, source_target_pairs={{0,1},{1,0},{2,3},{3,2},{4,5},{5,4},{6,7},{7,6},{8,9},{9,8},{10,11... | collective-permute-start | bytes 663560 | tf_op jit(solution)/shard_map/ppermute | solution.py:24
  88.5 14.9 %collective-permute-start.14 = (f16[96,1152]{1,0:T(8,128)(2,1)S(1)}, f16[96,1152]{1,0:T(8,128)(2,1)S(1)}, u32[]{:S(2)}, u32[]{:S(2)}) collective-permute-start(f16[96,1152]{1,0:T(8,128)(2,1)S(1)} %convert_element_type.56), channel_id=1, source_target_pairs={{0,2},{1,3},{2,0},{3,1},{4,6},{5,7},{6,4},{7,5},{8,10},{9,11},{10,... | collective-permute-start | bytes 663560 | tf_op jit(solution)/shard_map/ppermute | solution.py:24
  90.5 20.3 %collective-permute-start.9 = (f16[96,1152]{1,0:T(8,128)(2,1)S(1)}, f16[96,1152]{1,0:T(8,128)(2,1)S(1)}, u32[]{:S(2)}, u32[]{:S(2)}) collective-permute-start(f16[96,1152]{1,0:T(8,128)(2,1)S(1)} %convert_element_type.46), channel_id=1, source_target_pairs={{0,1},{1,0},{2,3},{3,2},{4,5},{5,4},{6,7},{7,6},{8,9},{9,8},{10,11... | collective-permute-start | bytes 663560 | tf_op jit(solution)/shard_map/ppermute | solution.py:24
  100.5 21.6 %collective-permute-start.11 = (f16[96,1152]{1,0:T(8,128)(2,1)S(1)}, f16[96,1152]{1,0:T(8,128)(2,1)S(1)}, u32[]{:S(2)}, u32[]{:S(2)}) collective-permute-start(f16[96,1152]{1,0:T(8,128)(2,1)S(1)} %convert_element_type.50), channel_id=1, source_target_pairs={{0,2},{1,3},{2,0},{3,1},{4,6},{5,7},{6,4},{7,5},{8,10},{9,11},{10,... | collective-permute-start | bytes 663560 | tf_op jit(solution)/shard_map/ppermute | solution.py:24
  103.7 26.4 %collective-permute-start.15 = (f16[96,1152]{1,0:T(8,128)(2,1)S(1)}, f16[96,1152]{1,0:T(8,128)(2,1)S(1)}, u32[]{:S(2)}, u32[]{:S(2)}) collective-permute-start(f16[96,1152]{1,0:T(8,128)(2,1)S(1)} %convert_element_type.58), channel_id=1, source_target_pairs={{0,4},{1,5},{2,6},{3,7},{4,0},{5,1},{6,2},{7,3},{8,12},{9,13},{10,... | collective-permute-start | bytes 663560 | tf_op jit(solution)/shard_map/ppermute | solution.py:24
Sparse Core Ops, SparseCore 0:
  9.5 51.6 all-gather.1

commit v5 on v4

--- a/solution.py
+++ b/solution.py
@@ -95,13 +95,14 @@
             grads_ref[slot, k * 96:(k + 1) * 96, :] = turned[pl.ds(pl.multiple_of(first, 32), 96), :]
 
 
-def spread(at_ref, own, other, acts_ref, sems):
+def spread(at_ref, own, other, acts_ref, sems, lo=0, hi=1136, sem=0):
     x, core = at_ref[1], at_ref[2]
     copies = []
     for xr in range(4):
         slot = lax.rem(x + xr, 4) * 256
         for i, (src, c) in enumerate(((own, core), (other, 1 - core))):
-            copies.append(pltpu.make_async_copy(src.at[xr], acts_ref.at[:, lanes_at(slot + c * 128, 128)], sems.at[2 * xr + i]))
+            copies.append(pltpu.make_async_copy(
+                src.at[xr, lo:hi, :], acts_ref.at[lo:hi, lanes_at(slot + c * 128, 128)], sems.at[sem + 2 * xr + i]))
     for copy in copies:
         copy.start()
     return copies
@@ -127,11 +128,12 @@
 
 def rest_kernel(at_ref, s1, t1, grads_ref, start_ref, *refs):
     far0_ref, far1_ref, near0_ref, near1_ref, keep_far_ref, keep_near_ref, acts_ref, sems = refs
-    for copy in spread(at_ref, s1, t1, acts_ref, sems):
-        copy.wait()
+    arriving = [spread(at_ref, s1, t1, acts_ref, sems, lo, hi, 8 * i) for i, (lo, hi) in enumerate(TILES)]
     places = ((far0_ref, 0), (far1_ref, 96), (keep_far_ref, 192), (near0_ref, 384), (near1_ref, 480), (keep_near_ref, 576))
     tops = []
-    for lo, hi in TILES:
+    for (lo, hi), copies in zip(TILES, arriving):
+        for copy in copies:
+            copy.wait()
         part = start_ref[:, lo:hi] + sum(
             lax.dot_general(grads_ref[2 + j], acts_ref[lo:hi, j * 512:(j + 1) * 512], NT, preferred_element_type=f32) for j in range(2))
         for ref, first in places:
@@ -190,13 +192,13 @@
     x1, x2, x3, swapped, token = tie(x1, x2, x3, swapped, token)
     s0 = jnp.stack([bt, x1, x2, x3])
     t0 = other_core(s0)
-    o1, o2, o3 = (over_x(swapped, s) for s in (1, 2, 3))
+    o2, o1, o3 = (over_x(swapped, s) for s in (2, 1, 3))
     grads = pl.pallas_call(
         prep_kernel, out_shape=shape((4, 768, 512), bf16),
         in_specs=[SM, ANY], out_specs=VM, compiler_params=PARAMS, name="prep",
         scratch_shapes=[pltpu.VMEM((4, 512, 768), bf16), pltpu.VMEM((768, 512), bf16), pltpu.SemaphoreType.DMA((4,))],
     )(where, every_grad)
-    o1, o2, o3, grads = tie(o1, o2, o3, grads)
+    o2, o1, o3, grads = tie(o2, o1, o3, grads)
     s1 = jnp.stack([swapped, o1, o2, o3])
     t1 = other_core(s1)
     t0, s1 = tie(t0, s1)
@@ -209,7 +211,7 @@
     *sends, keep_far, keep_near = pl.pallas_call(
         rest_kernel, out_shape=(shape((96, 1152), f32),) * 4 + (shape((192, 1152), f32),) * 2,
         in_specs=[SM] + [ANY] * 2 + [VM] * 2, out_specs=(VM,) * 6, compiler_params=PARAMS, name="rest",
-        scratch_shapes=[pltpu.VMEM((1136, 1024), bf16), pltpu.SemaphoreType.DMA((8,))],
+        scratch_shapes=[pltpu.VMEM((1136, 1024), bf16), pltpu.SemaphoreType.DMA((40,))],
     )(where, s1, t1, grads, start)
     f0, f1, n0, n1 = (depth_pair(m.astype(f16), 1) for m in sends)
     (f2,) = stage(keep_far[:96], f0, (0, 96, True))

time: 139 us -> 141 us (1.014)
  Pallas kernels: 12 us -> 14.8 us
  starting transfers between devices: 67.7 us -> 65.6 us
  waiting for transfers between devices: 40.7 us -> 42.8 us
    pallas_call x1, Pallas kernels: 3.94 us -> 6.77 us  [body(): pl.pallas_call(rest_kernel, out_shape=(shape((96, 1152), f32),) * 4 + (sh...]
    ppermute x16, starting transfers between devices: 67.7 us -> 65.6 us  [permute(): return lax.ppermute(value, AXES, pairs)]
    ppermute x16, waiting for transfers between devices: 35.9 us -> 37.3 us  [permute(): return lax.ppermute(value, AXES, pairs)]
where the time goes in v5:
time: 141 us
  starting transfers between devices  65.6 us (47%)
  waiting for transfers between devices  42.8 us (30%)
  Pallas kernels  14.8 us (10%)
  between operations  13.8 us (10%)
  local copies, waits for them, and re-layouts  2.1 us (1%)
  other arithmetic  1.67 us (1%)
    ppermute x16, starting transfers between devices, permute(): return lax.ppermute(value, AXES, pairs)  65.6 us
    ppermute x16, waiting for transfers between devices, permute(): return lax.ppermute(value, AXES, pairs)  37.3 us
    pallas_call x1, Pallas kernels, body(): pl.pallas_call(rest_kernel, out_shape=(shape((96, 1152), f32),) * 4 + (sh...  6.77 us
    all_gather x1, waiting for transfers between devices, body(): every_grad = lax.all_gather(out_grads, 'col', axis=0, tiled=True)  4.77 us
    pallas_call x1, Pallas kernels, body(): pl.pallas_call(own_kernel, out_shape=shape((768, 1136), f32), in_specs=[S...  3.55 us
  transfers between devices with their start and end apart: 17, of which 9 were waited for; matrix products, arithmetic and copies ran while one was open for 1% of the time, Pallas kernels for 5%

profile of v5, /device:TPU:2, one launch (start us, length us, event | category | flops | bytes accessed | tf_op | source)
XLA Modules:
  0.0 140.8 jit_solution(13555801900338210536)
XLA Ops:
  7.3 15.7 %collective-permute-start.3 = (bf16[1136,128]{1,0:T(8,128)(2,1)}, bf16[1136,128]{1,0:T(8,128)(2,1)S(1)}, u32[]{:S(2)}, u32[]{:S(2)}) collective-permute-start(bf16[1136,128]{1,0:T(8,128)(2,1)} %bitcast.14), channel_id=1, source_target_pairs={{0,256},{1,257},{2,258},{3,259},{4,260},{5,261},{6,262},{7,263},{8... | collective-permute-start | bytes 872456 | tf_op jit(solution)/shard_map/ppermute | solution.py:24
  23.0 3.4 %collective-permute-start.2 = (bf16[1136,128]{1,0:T(8,128)(2,1)}, bf16[1136,128]{1,0:T(8,128)(2,1)S(1)}, u32[]{:S(2)}, u32[]{:S(2)}) collective-permute-start(bf16[1136,128]{1,0:T(8,128)(2,1)} %bitcast.15), channel_id=1, source_target_pairs={{0,64},{1,65},{2,66},{3,67},{4,68},{5,69},{6,70},{7,71},{8,72},{9,... | collective-permute-start | bytes 872456 | tf_op jit(solution)/shard_map/ppermute | solution.py:24
  26.4 3.0 %collective-permute-start.1 = (bf16[1136,128]{1,0:T(8,128)(2,1)}, bf16[1136,128]{1,0:T(8,128)(2,1)S(1)}, u32[]{:S(2)}, u32[]{:S(2)}) collective-permute-start(bf16[1136,128]{1,0:T(8,128)(2,1)} %bitcast.16), channel_id=1, source_target_pairs={{0,128},{1,129},{2,130},{3,131},{4,132},{5,133},{6,134},{7,135},{8... | collective-permute-start | bytes 872456 | tf_op jit(solution)/shard_map/ppermute | solution.py:24
  29.5 4.1 %collective-permute-start = (bf16[1136,128]{1,0:T(8,128)(2,1)}, bf16[1136,128]{1,0:T(8,128)(2,1)S(1)}, u32[]{:S(2)}, u32[]{:S(2)}) collective-permute-start(bf16[1136,128]{1,0:T(8,128)(2,1)} %bitcast.17), channel_id=1, source_target_pairs={{0,192},{1,193},{2,194},{3,195},{4,196},{5,197},{6,198},{7,199},{8... | collective-permute-start | bytes 872456 | tf_op jit(solution)/shard_map/ppermute | solution.py:24
  35.0 5.0 %collective-permute-done.1 = bf16[1136,128]{1,0:T(8,128)(2,1)S(1)} collective-permute-done((bf16[1136,128]{1,0:T(8,128)(2,1)}, bf16[1136,128]{1,0:T(8,128)(2,1)S(1)}, u32[]{:S(2)}, u32[]{:S(2)}) %collective-permute-start.1) | collective-permute-done | bytes 290848 | tf_op jit(solution)/shard_map/ppermute | solution.py:24
  39.9 4.4 %collective-permute-done = bf16[1136,128]{1,0:T(8,128)(2,1)S(1)} collective-permute-done((bf16[1136,128]{1,0:T(8,128)(2,1)}, bf16[1136,128]{1,0:T(8,128)(2,1)S(1)}, u32[]{:S(2)}, u32[]{:S(2)}) %collective-permute-start) | collective-permute-done | bytes 290848 | tf_op jit(solution)/shard_map/ppermute | solution.py:24
  44.4 2.5 %collective-permute-start.7 = (bf16[1136,128]{1,0:T(8,128)(2,1)S(1)}, bf16[1136,128]{1,0:T(8,128)(2,1)S(1)}, u32[]{:S(2)}, u32[]{:S(2)}) collective-permute-start(bf16[1136,128]{1,0:T(8,128)(2,1)S(1)} %collective-permute-done.3), channel_id=1, source_target_pairs={{0,64},{1,65},{2,66},{3,67},{4,68},{5,69},{6,70},{7,71},{8,72},{9,... | collective-permute-start | bytes 872456 | tf_op jit(solution)/shard_map/ppermute | solution.py:24
  46.9 3.3 %collective-permute-start.6 = (bf16[1136,128]{1,0:T(8,128)(2,1)S(1)}, bf16[1136,128]{1,0:T(8,128)(2,1)S(1)}, u32[]{:S(2)}, u32[]{:S(2)}) collective-permute-start(bf16[1136,128]{1,0:T(8,128)(2,1)S(1)} %collective-permute-done.3), channel_id=1, source_target_pairs={{0,192},{1,193},{2,194},{3,195},{4,196},{5,197},{6,198},{7,199},{8... | collective-permute-start | bytes 872456 | tf_op jit(solution)/shard_map/ppermute | solution.py:24
  50.2 3.0 %collective-permute-start.5 = (bf16[1136,128]{1,0:T(8,128)(2,1)S(1)}, bf16[1136,128]{1,0:T(8,128)(2,1)S(1)}, u32[]{:S(2)}, u32[]{:S(2)}) collective-permute-start(bf16[1136,128]{1,0:T(8,128)(2,1)S(1)} %collective-permute-done.3), channel_id=1, source_target_pairs={{0,128},{1,129},{2,130},{3,131},{4,132},{5,133},{6,134},{7,135},{8... | collective-permute-start | bytes 872456 | tf_op jit(solution)/shard_map/ppermute | solution.py:24
  54.5 1.9 %collective-permute-start.4 = (bf16[4,1136,128]{2,1,0:T(8,128)(2,1)S(1)}, bf16[4,1136,128]{2,1,0:T(8,128)(2,1)S(1)}, u32[]{:S(2)}, u32[]{:S(2)}) collective-permute-start(bf16[4,1136,128]{2,1,0:T(8,128)(2,1)S(1)} %pad_maximum_fusion.s0), channel_id=1, source_target_pairs={{0,32},{1,33},{2,34},{3,35},{4,36},{5,37},{6,38},{7,39},{8,40},{9,... | collective-permute-start | bytes 3489800 | tf_op jit(solution)/shard_map/ppermute | solution.py:24
  56.4 4.8 %all-gather.2.cloned.1.call-done.all_ref = bf16[2048,768]{1,0:T(8,128)(2,1)} async-done(((bf16[512,768]{1,0:T(8,128)(2,1)}), bf16[2048,768]{1,0:T(8,128)(2,1)}) %all-gather.2.cloned.1.call-update) | async-done | bytes 3145744 | tf_op jit(solution)/shard_map/all_gather | solution.py:186
  63.1 2.0 %prep.1.grads_ref = bf16[4,768,512]{2,1,0:T(8,128)(2,1)S(1)} custom-call(s32[5]{0:T(128)S(1)} %stack.53.at_ref, bf16[2048,768]{1,0:T(8,128)(2,1)S(1)} %copy-done), custom_call_target="tpu_custom_call" | custom-call | tf_op jit(solution)/shard_map/prep/pallas_call | solution.py:196
  65.3 1.9 %collective-permute-start.8 = (bf16[4,1136,128]{2,1,0:T(8,128)(2,1)S(1)}, bf16[4,1136,128]{2,1,0:T(8,128)(2,1)S(1)}, u32[]{:S(2)}, u32[]{:S(2)}) collective-permute-start(bf16[4,1136,128]{2,1,0:T(8,128)(2,1)S(1)} %pad_maximum_fusion.1.s1), channel_id=1, source_target_pairs={{0,32},{1,33},{2,34},{3,35},{4,36},{5,37},{6,38},{7,39},{8,40},{9,... | collective-permute-start | bytes 3489800 | tf_op jit(solution)/shard_map/ppermute | solution.py:24
  67.3 3.6 %own.1.start_ref = f32[768,1136]{1,0:T(8,128)S(1)} custom-call(s32[5]{0:T(128)S(1)} %stack.53.at_ref, bf16[4,1136,128]{2,1,0:T(8,128)(2,1)S(1)} %pad_maximum_fusion.s0, bf16[4,1136,128]{2,1,0:T(8,128)(2,1)S(1)} %collective-permute-done.4.t0, bf16[4,768,512]{2,1,0:T(8,128)(2,1)S(1)} %prep.1.grads_ref, f32[8,128]{1,0:T(8,128)S(1)} %fence.3.token), custom_call_target="tpu_custom_call" | custom-call | tf_op jit(solution)/shard_map/own/pallas_call | solution.py:205
  70.8 6.8 %rest.1 = (f32[96,1152]{1,0:T(8,128)S(1)}, f32[96,1152]{1,0:T(8,128)S(1)}, f32[96,1152]{1,0:T(8,128)S(1)}, f32[96,1152]{1,0:T(8,128)S(1)}, f32[192,1152]{1,0:T(8,128)S(1)}, /*index=5*/f32[192,1152]{1,0:T(8,128)S(1)}) custom-call(s32[5]{0:T(128)S(1)} %stack.53.at_ref, bf16[4,1136,128]{2,1,0:T(8,128)(2,1)S(1)} %pad_maximum_fusion.1.s1, ...), custom_call_target="tpu_custom_call" | custom-call | tf_op jit(solution)/shard_map/rest/pallas_call | solution.py:211
  77.7 6.1 %collective-permute-start.13 = (f16[96,1152]{1,0:T(8,128)(2,1)S(1)}, f16[96,1152]{1,0:T(8,128)(2,1)S(1)}, u32[]{:S(2)}, u32[]{:S(2)}) collective-permute-start(f16[96,1152]{1,0:T(8,128)(2,1)S(1)} %convert_element_type.54), channel_id=1, source_target_pairs={{0,1},{1,0},{2,3},{3,2},{4,5},{5,4},{6,7},{7,6},{8,9},{9,8},{10,11... | collective-permute-start | bytes 663560 | tf_op jit(solution)/shard_map/ppermute | solution.py:24
  85.8 3.9 %collective-permute-start.10 = (f16[96,1152]{1,0:T(8,128)(2,1)S(1)}, f16[96,1152]{1,0:T(8,128)(2,1)S(1)}, u32[]{:S(2)}, u32[]{:S(2)}) collective-permute-start(f16[96,1152]{1,0:T(8,128)(2,1)S(1)} %convert_element_type.48), channel_id=1, source_target_pairs={{0,1},{1,0},{2,3},{3,2},{4,5},{5,4},{6,7},{7,6},{8,9},{9,8},{10,11... | collective-permute-start | bytes 663560 | tf_op jit(solution)/shard_map/ppermute | solution.py:24
  90.4 2.2 %collective-permute-start.14 = (f16[96,1152]{1,0:T(8,128)(2,1)S(1)}, f16[96,1152]{1,0:T(8,128)(2,1)S(1)}, u32[]{:S(2)}, u32[]{:S(2)}) collective-permute-start(f16[96,1152]{1,0:T(8,128)(2,1)S(1)} %convert_element_type.56), channel_id=1, source_target_pairs={{0,2},{1,3},{2,0},{3,1},{4,6},{5,7},{6,4},{7,5},{8,10},{9,11},{10,... | collective-permute-start | bytes 663560 | tf_op jit(solution)/shard_map/ppermute | solution.py:24
  92.7 3.6 %collective-permute-start.9 = (f16[96,1152]{1,0:T(8,128)(2,1)S(1)}, f16[96,1152]{1,0:T(8,128)(2,1)S(1)}, u32[]{:S(2)}, u32[]{:S(2)}) collective-permute-start(f16[96,1152]{1,0:T(8,128)(2,1)S(1)} %convert_element_type.46), channel_id=1, source_target_pairs={{0,1},{1,0},{2,3},{3,2},{4,5},{5,4},{6,7},{7,6},{8,9},{9,8},{10,11... | collective-permute-start | bytes 663560 | tf_op jit(solution)/shard_map/ppermute | solution.py:24
  96.2 6.7 %collective-permute-done.10 = f16[96,1152]{1,0:T(8,128)(2,1)S(1)} collective-permute-done((f16[96,1152]{1,0:T(8,128)(2,1)S(1)}, f16[96,1152]{1,0:T(8,128)(2,1)S(1)}, u32[]{:S(2)}, u32[]{:S(2)}) %collective-permute-start.10) | collective-permute-done | bytes 221216 | tf_op jit(solution)/shard_map/ppermute | solution.py:24
  103.3 2.6 %collective-permute-start.11 = (f16[96,1152]{1,0:T(8,128)(2,1)S(1)}, f16[96,1152]{1,0:T(8,128)(2,1)S(1)}, u32[]{:S(2)}, u32[]{:S(2)}) collective-permute-start(f16[96,1152]{1,0:T(8,128)(2,1)S(1)} %convert_element_type.50), channel_id=1, source_target_pairs={{0,2},{1,3},{2,0},{3,1},{4,6},{5,7},{6,4},{7,5},{8,10},{9,11},{10,... | collective-permute-start | bytes 663560 | tf_op jit(solution)/shard_map/ppermute | solution.py:24
  106.5 6.4 %collective-permute-start.15 = (f16[96,1152]{1,0:T(8,128)(2,1)S(1)}, f16[96,1152]{1,0:T(8,128)(2,1)S(1)}, u32[]{:S(2)}, u32[]{:S(2)}) collective-permute-start(f16[96,1152]{1,0:T(8,128)(2,1)S(1)} %convert_element_type.58), channel_id=1, source_target_pairs={{0,4},{1,5},{2,6},{3,7},{4,0},{5,1},{6,2},{7,3},{8,12},{9,13},{10,... | collective-permute-start | bytes 663560 | tf_op jit(solution)/shard_map/ppermute | solution.py:24
  113.2 11.2 %collective-permute-done.11 = f16[96,1152]{1,0:T(8,128)(2,1)S(1)} collective-permute-done((f16[96,1152]{1,0:T(8,128)(2,1)S(1)}, f16[96,1152]{1,0:T(8,128)(2,1)S(1)}, u32[]{:S(2)}, u32[]{:S(2)}) %collective-permute-start.11) | collective-permute-done | bytes 221216 | tf_op jit(solution)/shard_map/ppermute | solution.py:24
  124.7 8.2 %collective-permute-done.15 = f16[96,1152]{1,0:T(8,128)(2,1)S(1)} collective-permute-done((f16[96,1152]{1,0:T(8,128)(2,1)S(1)}, f16[96,1152]{1,0:T(8,128)(2,1)S(1)}, u32[]{:S(2)}, u32[]{:S(2)}) %collective-permute-start.15) | collective-permute-done | bytes 221216 | tf_op jit(solution)/shard_map/ppermute | solution.py:24
  (44 shorter events, 10.6 us)
Async XLA Ops:
  6.5 54.7 %all-gather.2.cloned.1.call-start = ((), (), s32[]{:S(2)}) async-start(), calls=%async_computation | async-start | bytes 3932160 | tf_op jit(solution)/shard_map/all_gather | solution.py:186
  7.3 27.4 %collective-permute-start.3 = (bf16[1136,128]{1,0:T(8,128)(2,1)}, bf16[1136,128]{1,0:T(8,128)(2,1)S(1)}, u32[]{:S(2)}, u32[]{:S(2)}) collective-permute-start(bf16[1136,128]{1,0:T(8,128)(2,1)} %bitcast.14), channel_id=1, source_target_pairs={{0,256},{1,257},{2,258},{3,259},{4,260},{5,261},{6,262},{7,263},{8... | collective-permute-start | bytes 872456 | tf_op jit(solution)/shard_map/ppermute | solution.py:24
  23.0 12.0 %collective-permute-start.2 = (bf16[1136,128]{1,0:T(8,128)(2,1)}, bf16[1136,128]{1,0:T(8,128)(2,1)S(1)}, u32[]{:S(2)}, u32[]{:S(2)}) collective-permute-start(bf16[1136,128]{1,0:T(8,128)(2,1)} %bitcast.15), channel_id=1, source_target_pairs={{0,64},{1,65},{2,66},{3,67},{4,68},{5,69},{6,70},{7,71},{8,72},{9,... | collective-permute-start | bytes 872456 | tf_op jit(solution)/shard_map/ppermute | solution.py:24
  26.4 13.5 %collective-permute-start.1 = (bf16[1136,128]{1,0:T(8,128)(2,1)}, bf16[1136,128]{1,0:T(8,128)(2,1)S(1)}, u32[]{:S(2)}, u32[]{:S(2)}) collective-permute-start(bf16[1136,128]{1,0:T(8,128)(2,1)} %bitcast.16), channel_id=1, source_target_pairs={{0,128},{1,129},{2,130},{3,131},{4,132},{5,133},{6,134},{7,135},{8... | collective-permute-start | bytes 872456 | tf_op jit(solution)/shard_map/ppermute | solution.py:24
  29.5 14.9 %collective-permute-start = (bf16[1136,128]{1,0:T(8,128)(2,1)}, bf16[1136,128]{1,0:T(8,128)(2,1)S(1)}, u32[]{:S(2)}, u32[]{:S(2)}) collective-permute-start(bf16[1136,128]{1,0:T(8,128)(2,1)} %bitcast.17), channel_id=1, source_target_pairs={{0,192},{1,193},{2,194},{3,195},{4,196},{5,197},{6,198},{7,199},{8... | collective-permute-start | bytes 872456 | tf_op jit(solution)/shard_map/ppermute | solution.py:24
  44.4 20.8 %collective-permute-start.7 = (bf16[1136,128]{1,0:T(8,128)(2,1)S(1)}, bf16[1136,128]{1,0:T(8,128)(2,1)S(1)}, u32[]{:S(2)}, u32[]{:S(2)}) collective-permute-start(bf16[1136,128]{1,0:T(8,128)(2,1)S(1)} %collective-permute-done.3), channel_id=1, source_target_pairs={{0,64},{1,65},{2,66},{3,67},{4,68},{5,69},{6,70},{7,71},{8,72},{9,... | collective-permute-start | bytes 872456 | tf_op jit(solution)/shard_map/ppermute | solution.py:24
  46.9 18.3 %collective-permute-start.6 = (bf16[1136,128]{1,0:T(8,128)(2,1)S(1)}, bf16[1136,128]{1,0:T(8,128)(2,1)S(1)}, u32[]{:S(2)}, u32[]{:S(2)}) collective-permute-start(bf16[1136,128]{1,0:T(8,128)(2,1)S(1)} %collective-permute-done.3), channel_id=1, source_target_pairs={{0,192},{1,193},{2,194},{3,195},{4,196},{5,197},{6,198},{7,199},{8... | collective-permute-start | bytes 872456 | tf_op jit(solution)/shard_map/ppermute | solution.py:24
  50.2 14.9 %collective-permute-start.5 = (bf16[1136,128]{1,0:T(8,128)(2,1)S(1)}, bf16[1136,128]{1,0:T(8,128)(2,1)S(1)}, u32[]{:S(2)}, u32[]{:S(2)}) collective-permute-start(bf16[1136,128]{1,0:T(8,128)(2,1)S(1)} %collective-permute-done.3), channel_id=1, source_target_pairs={{0,128},{1,129},{2,130},{3,131},{4,132},{5,133},{6,134},{7,135},{8... | collective-permute-start | bytes 872456 | tf_op jit(solution)/shard_map/ppermute | solution.py:24
  54.5 12.8 %collective-permute-start.4 = (bf16[4,1136,128]{2,1,0:T(8,128)(2,1)S(1)}, bf16[4,1136,128]{2,1,0:T(8,128)(2,1)S(1)}, u32[]{:S(2)}, u32[]{:S(2)}) collective-permute-start(bf16[4,1136,128]{2,1,0:T(8,128)(2,1)S(1)} %pad_maximum_fusion.s0), channel_id=1, source_target_pairs={{0,32},{1,33},{2,34},{3,35},{4,36},{5,37},{6,38},{7,39},{8,40},{9,... | collective-permute-start | bytes 3489800 | tf_op jit(solution)/shard_map/ppermute | solution.py:24
  61.2 1.9 %copy-start = (bf16[2048,768]{1,0:T(8,128)(2,1)S(1)}, bf16[2048,768]{1,0:T(8,128)(2,1)}, u32[]{:S(2)}) copy-start(bf16[2048,768]{1,0:T(8,128)(2,1)} %all-gather.2.cloned.1.call-done.all_ref) | copy-start | bytes 9437188
  65.3 5.5 %collective-permute-start.8 = (bf16[4,1136,128]{2,1,0:T(8,128)(2,1)S(1)}, bf16[4,1136,128]{2,1,0:T(8,128)(2,1)S(1)}, u32[]{:S(2)}, u32[]{:S(2)}) collective-permute-start(bf16[4,1136,128]{2,1,0:T(8,128)(2,1)S(1)} %pad_maximum_fusion.1.s1), channel_id=1, source_target_pairs={{0,32},{1,33},{2,34},{3,35},{4,36},{5,37},{6,38},{7,39},{8,40},{9,... | collective-permute-start | bytes 3489800 | tf_op jit(solution)/shard_map/ppermute | solution.py:24
  77.7 12.4 %collective-permute-start.13 = (f16[96,1152]{1,0:T(8,128)(2,1)S(1)}, f16[96,1152]{1,0:T(8,128)(2,1)S(1)}, u32[]{:S(2)}, u32[]{:S(2)}) collective-permute-start(f16[96,1152]{1,0:T(8,128)(2,1)S(1)} %convert_element_type.54), channel_id=1, source_target_pairs={{0,1},{1,0},{2,3},{3,2},{4,5},{5,4},{6,7},{7,6},{8,9},{9,8},{10,11... | collective-permute-start | bytes 663560 | tf_op jit(solution)/shard_map/ppermute | solution.py:24
  83.8 22.1 %collective-permute-start.12 = (f16[96,1152]{1,0:T(8,128)(2,1)S(1)}, f16[96,1152]{1,0:T(8,128)(2,1)S(1)}, u32[]{:S(2)}, u32[]{:S(2)}) collective-permute-start(f16[96,1152]{1,0:T(8,128)(2,1)S(1)} %convert_element_type.52), channel_id=1, source_target_pairs={{0,1},{1,0},{2,3},{3,2},{4,5},{5,4},{6,7},{7,6},{8,9},{9,8},{10,11... | collective-permute-start | bytes 663560 | tf_op jit(solution)/shard_map/ppermute | solution.py:24
  85.8 17.2 %collective-permute-start.10 = (f16[96,1152]{1,0:T(8,128)(2,1)S(1)}, f16[96,1152]{1,0:T(8,128)(2,1)S(1)}, u32[]{:S(2)}, u32[]{:S(2)}) collective-permute-start(f16[96,1152]{1,0:T(8,128)(2,1)S(1)} %convert_element_type.48), channel_id=1, source_target_pairs={{0,1},{1,0},{2,3},{3,2},{4,5},{5,4},{6,7},{7,6},{8,9},{9,8},{10,11... | collective-permute-start | bytes 663560 | tf_op jit(solution)/shard_map/ppermute | solution.py:24
  90.4 15.7 %collective-permute-start.14 = (f16[96,1152]{1,0:T(8,128)(2,1)S(1)}, f16[96,1152]{1,0:T(8,128)(2,1)S(1)}, u32[]{:S(2)}, u32[]{:S(2)}) collective-permute-start(f16[96,1152]{1,0:T(8,128)(2,1)S(1)} %convert_element_type.56), channel_id=1, source_target_pairs={{0,2},{1,3},{2,0},{3,1},{4,6},{5,7},{6,4},{7,5},{8,10},{9,11},{10,... | collective-permute-start | bytes 663560 | tf_op jit(solution)/shard_map/ppermute | solution.py:24
  92.7 20.3 %collective-permute-start.9 = (f16[96,1152]{1,0:T(8,128)(2,1)S(1)}, f16[96,1152]{1,0:T(8,128)(2,1)S(1)}, u32[]{:S(2)}, u32[]{:S(2)}) collective-permute-start(f16[96,1152]{1,0:T(8,128)(2,1)S(1)} %convert_element_type.46), channel_id=1, source_target_pairs={{0,1},{1,0},{2,3},{3,2},{4,5},{5,4},{6,7},{7,6},{8,9},{9,8},{10,11... | collective-permute-start | bytes 663560 | tf_op jit(solution)/shard_map/ppermute | solution.py:24
  103.3 21.2 %collective-permute-start.11 = (f16[96,1152]{1,0:T(8,128)(2,1)S(1)}, f16[96,1152]{1,0:T(8,128)(2,1)S(1)}, u32[]{:S(2)}, u32[]{:S(2)}) collective-permute-start(f16[96,1152]{1,0:T(8,128)(2,1)S(1)} %convert_element_type.50), channel_id=1, source_target_pairs={{0,2},{1,3},{2,0},{3,1},{4,6},{5,7},{6,4},{7,5},{8,10},{9,11},{10,... | collective-permute-start | bytes 663560 | tf_op jit(solution)/shard_map/ppermute | solution.py:24
  106.5 26.4 %collective-permute-start.15 = (f16[96,1152]{1,0:T(8,128)(2,1)S(1)}, f16[96,1152]{1,0:T(8,128)(2,1)S(1)}, u32[]{:S(2)}, u32[]{:S(2)}) collective-permute-start(f16[96,1152]{1,0:T(8,128)(2,1)S(1)} %convert_element_type.58), channel_id=1, source_target_pairs={{0,4},{1,5},{2,6},{3,7},{4,0},{5,1},{6,2},{7,3},{8,12},{9,13},{10,... | collective-permute-start | bytes 663560 | tf_op jit(solution)/shard_map/ppermute | solution.py:24
Sparse Core Ops, SparseCore 0:
  9.5 51.6 all-gather.1

commit v6 on v4

--- a/solution.py
+++ b/solution.py
@@ -193,7 +193,7 @@
     o1, o2, o3 = (over_x(swapped, s) for s in (1, 2, 3))
     grads = pl.pallas_call(
         prep_kernel, out_shape=shape((4, 768, 512), bf16),
-        in_specs=[SM, ANY], out_specs=VM, compiler_params=PARAMS, name="prep",
+        in_specs=[SM, pl.BlockSpec(memory_space=pltpu.HBM)], out_specs=VM, compiler_params=PARAMS, name="prep",
         scratch_shapes=[pltpu.VMEM((4, 512, 768), bf16), pltpu.VMEM((768, 512), bf16), pltpu.SemaphoreType.DMA((4,))],
     )(where, every_grad)
     o1, o2, o3, grads = tie(o1, o2, o3, grads)

time: 139 us -> 139 us (level)
  no operation moved by 1% of the time
where the time goes in v6:
time: 139 us; the launch traced here: 138 us
  starting transfers between devices  67.7 us (49%)
  waiting for transfers between devices  40.7 us (29%)
  between operations  13.8 us (10%)
  Pallas kernels  12 us (9%)
  local copies, waits for them, and re-layouts  2.1 us (2%)
  other arithmetic  1.67 us (1%)
    ppermute x16, starting transfers between devices, permute(): return lax.ppermute(value, AXES, pairs)  67.7 us
    ppermute x16, waiting for transfers between devices, permute(): return lax.ppermute(value, AXES, pairs)  35.9 us
    all_gather x1, waiting for transfers between devices, body(): every_grad = lax.all_gather(out_grads, 'col', axis=0, tiled=True)  4.17 us
    pallas_call x1, Pallas kernels, body(): pl.pallas_call(rest_kernel, out_shape=(shape((96, 1152), f32),) * 4 + (sh...  3.94 us
    pallas_call x1, Pallas kernels, body(): pl.pallas_call(own_kernel, out_shape=shape((768, 1136), f32), in_specs=[S...  3.55 us
  transfers between devices with their start and end apart: 17, of which 9 were waited for; matrix products, arithmetic and copies ran while one was open for 1% of the time, Pallas kernels for 5%

profile of v6, /device:TPU:2, one launch (start us, length us, event | category | flops | bytes accessed | tf_op | source)
XLA Modules:
  0.0 138.0 jit_solution(11057665274311135009)
XLA Ops:
  7.3 15.7 %collective-permute-start.3 = (bf16[1136,128]{1,0:T(8,128)(2,1)}, bf16[1136,128]{1,0:T(8,128)(2,1)S(1)}, u32[]{:S(2)}, u32[]{:S(2)}) collective-permute-start(bf16[1136,128]{1,0:T(8,128)(2,1)} %bitcast.14), channel_id=1, source_target_pairs={{0,256},{1,257},{2,258},{3,259},{4,260},{5,261},{6,262},{7,263},{8... | collective-permute-start | bytes 872456 | tf_op jit(solution)/shard_map/ppermute | solution.py:24
  23.0 3.4 %collective-permute-start.2 = (bf16[1136,128]{1,0:T(8,128)(2,1)}, bf16[1136,128]{1,0:T(8,128)(2,1)S(1)}, u32[]{:S(2)}, u32[]{:S(2)}) collective-permute-start(bf16[1136,128]{1,0:T(8,128)(2,1)} %bitcast.15), channel_id=1, source_target_pairs={{0,64},{1,65},{2,66},{3,67},{4,68},{5,69},{6,70},{7,71},{8,72},{9,... | collective-permute-start | bytes 872456 | tf_op jit(solution)/shard_map/ppermute | solution.py:24
  26.4 3.0 %collective-permute-start.1 = (bf16[1136,128]{1,0:T(8,128)(2,1)}, bf16[1136,128]{1,0:T(8,128)(2,1)S(1)}, u32[]{:S(2)}, u32[]{:S(2)}) collective-permute-start(bf16[1136,128]{1,0:T(8,128)(2,1)} %bitcast.16), channel_id=1, source_target_pairs={{0,128},{1,129},{2,130},{3,131},{4,132},{5,133},{6,134},{7,135},{8... | collective-permute-start | bytes 872456 | tf_op jit(solution)/shard_map/ppermute | solution.py:24
  29.5 4.1 %collective-permute-start = (bf16[1136,128]{1,0:T(8,128)(2,1)}, bf16[1136,128]{1,0:T(8,128)(2,1)S(1)}, u32[]{:S(2)}, u32[]{:S(2)}) collective-permute-start(bf16[1136,128]{1,0:T(8,128)(2,1)} %bitcast.17), channel_id=1, source_target_pairs={{0,192},{1,193},{2,194},{3,195},{4,196},{5,197},{6,198},{7,199},{8... | collective-permute-start | bytes 872456 | tf_op jit(solution)/shard_map/ppermute | solution.py:24
  35.0 5.0 %collective-permute-done.1 = bf16[1136,128]{1,0:T(8,128)(2,1)S(1)} collective-permute-done((bf16[1136,128]{1,0:T(8,128)(2,1)}, bf16[1136,128]{1,0:T(8,128)(2,1)S(1)}, u32[]{:S(2)}, u32[]{:S(2)}) %collective-permute-start.1) | collective-permute-done | bytes 290848 | tf_op jit(solution)/shard_map/ppermute | solution.py:24
  39.9 4.4 %collective-permute-done = bf16[1136,128]{1,0:T(8,128)(2,1)S(1)} collective-permute-done((bf16[1136,128]{1,0:T(8,128)(2,1)}, bf16[1136,128]{1,0:T(8,128)(2,1)S(1)}, u32[]{:S(2)}, u32[]{:S(2)}) %collective-permute-start) | collective-permute-done | bytes 290848 | tf_op jit(solution)/shard_map/ppermute | solution.py:24
  44.4 2.5 %collective-permute-start.7 = (bf16[1136,128]{1,0:T(8,128)(2,1)S(1)}, bf16[1136,128]{1,0:T(8,128)(2,1)S(1)}, u32[]{:S(2)}, u32[]{:S(2)}) collective-permute-start(bf16[1136,128]{1,0:T(8,128)(2,1)S(1)} %collective-permute-done.3), channel_id=1, source_target_pairs={{0,64},{1,65},{2,66},{3,67},{4,68},{5,69},{6,70},{7,71},{8,72},{9,... | collective-permute-start | bytes 872456 | tf_op jit(solution)/shard_map/ppermute | solution.py:24
  46.9 3.0 %collective-permute-start.6 = (bf16[1136,128]{1,0:T(8,128)(2,1)S(1)}, bf16[1136,128]{1,0:T(8,128)(2,1)S(1)}, u32[]{:S(2)}, u32[]{:S(2)}) collective-permute-start(bf16[1136,128]{1,0:T(8,128)(2,1)S(1)} %collective-permute-done.3), channel_id=1, source_target_pairs={{0,128},{1,129},{2,130},{3,131},{4,132},{5,133},{6,134},{7,135},{8... | collective-permute-start | bytes 872456 | tf_op jit(solution)/shard_map/ppermute | solution.py:24
  49.9 4.0 %collective-permute-start.5 = (bf16[1136,128]{1,0:T(8,128)(2,1)S(1)}, bf16[1136,128]{1,0:T(8,128)(2,1)S(1)}, u32[]{:S(2)}, u32[]{:S(2)}) collective-permute-start(bf16[1136,128]{1,0:T(8,128)(2,1)S(1)} %collective-permute-done.3), channel_id=1, source_target_pairs={{0,192},{1,193},{2,194},{3,195},{4,196},{5,197},{6,198},{7,199},{8... | collective-permute-start | bytes 872456 | tf_op jit(solution)/shard_map/ppermute | solution.py:24
  55.1 1.9 %collective-permute-start.4 = (bf16[4,1136,128]{2,1,0:T(8,128)(2,1)S(1)}, bf16[4,1136,128]{2,1,0:T(8,128)(2,1)S(1)}, u32[]{:S(2)}, u32[]{:S(2)}) collective-permute-start(bf16[4,1136,128]{2,1,0:T(8,128)(2,1)S(1)} %pad_maximum_fusion.s0), channel_id=1, source_target_pairs={{0,32},{1,33},{2,34},{3,35},{4,36},{5,37},{6,38},{7,39},{8,40},{9,... | collective-permute-start | bytes 3489800 | tf_op jit(solution)/shard_map/ppermute | solution.py:24
  57.0 4.2 %all-gather.2.cloned.1.call-done.all_ref = bf16[2048,768]{1,0:T(8,128)(2,1)} async-done(((bf16[512,768]{1,0:T(8,128)(2,1)}), bf16[2048,768]{1,0:T(8,128)(2,1)}) %all-gather.2.cloned.1.call-update) | async-done | bytes 3145744 | tf_op jit(solution)/shard_map/all_gather | solution.py:184
  63.1 2.0 %prep.1.grads_ref = bf16[4,768,512]{2,1,0:T(8,128)(2,1)S(1)} custom-call(s32[5]{0:T(128)S(1)} %stack.53.at_ref, bf16[2048,768]{1,0:T(8,128)(2,1)S(1)} %copy-done), custom_call_target="tpu_custom_call" | custom-call | tf_op jit(solution)/shard_map/prep/pallas_call | solution.py:194
  65.3 1.9 %collective-permute-start.8 = (bf16[4,1136,128]{2,1,0:T(8,128)(2,1)S(1)}, bf16[4,1136,128]{2,1,0:T(8,128)(2,1)S(1)}, u32[]{:S(2)}, u32[]{:S(2)}) collective-permute-start(bf16[4,1136,128]{2,1,0:T(8,128)(2,1)S(1)} %pad_maximum_fusion.1.s1), channel_id=1, source_target_pairs={{0,32},{1,33},{2,34},{3,35},{4,36},{5,37},{6,38},{7,39},{8,40},{9,... | collective-permute-start | bytes 3489800 | tf_op jit(solution)/shard_map/ppermute | solution.py:24
  67.3 3.6 %own.1.start_ref = f32[768,1136]{1,0:T(8,128)S(1)} custom-call(s32[5]{0:T(128)S(1)} %stack.53.at_ref, bf16[4,1136,128]{2,1,0:T(8,128)(2,1)S(1)} %pad_maximum_fusion.s0, bf16[4,1136,128]{2,1,0:T(8,128)(2,1)S(1)} %collective-permute-done.4.t0, bf16[4,768,512]{2,1,0:T(8,128)(2,1)S(1)} %prep.1.grads_ref, f32[8,128]{1,0:T(8,128)S(1)} %fence.3.token), custom_call_target="tpu_custom_call" | custom-call | tf_op jit(solution)/shard_map/own/pallas_call | solution.py:203
  70.8 3.9 %rest.1 = (f32[96,1152]{1,0:T(8,128)S(1)}, f32[96,1152]{1,0:T(8,128)S(1)}, f32[96,1152]{1,0:T(8,128)S(1)}, f32[96,1152]{1,0:T(8,128)S(1)}, f32[192,1152]{1,0:T(8,128)S(1)}, /*index=5*/f32[192,1152]{1,0:T(8,128)S(1)}) custom-call(s32[5]{0:T(128)S(1)} %stack.53.at_ref, bf16[4,1136,128]{2,1,0:T(8,128)(2,1)S(1)} %pad_maximum_fusion.1.s1, ...), custom_call_target="tpu_custom_call" | custom-call | tf_op jit(solution)/shard_map/rest/pallas_call | solution.py:209
  74.9 7.0 %collective-permute-start.13 = (f16[96,1152]{1,0:T(8,128)(2,1)S(1)}, f16[96,1152]{1,0:T(8,128)(2,1)S(1)}, u32[]{:S(2)}, u32[]{:S(2)}) collective-permute-start(f16[96,1152]{1,0:T(8,128)(2,1)S(1)} %convert_element_type.54), channel_id=1, source_target_pairs={{0,1},{1,0},{2,3},{3,2},{4,5},{5,4},{6,7},{7,6},{8,9},{9,8},{10,11... | collective-permute-start | bytes 663560 | tf_op jit(solution)/shard_map/ppermute | solution.py:24
  81.9 1.9 %collective-permute-start.12 = (f16[96,1152]{1,0:T(8,128)(2,1)S(1)}, f16[96,1152]{1,0:T(8,128)(2,1)S(1)}, u32[]{:S(2)}, u32[]{:S(2)}) collective-permute-start(f16[96,1152]{1,0:T(8,128)(2,1)S(1)} %convert_element_type.52), channel_id=1, source_target_pairs={{0,1},{1,0},{2,3},{3,2},{4,5},{5,4},{6,7},{7,6},{8,9},{9,8},{10,11... | collective-permute-start | bytes 663560 | tf_op jit(solution)/shard_map/ppermute | solution.py:24
  83.8 3.9 %collective-permute-start.10 = (f16[96,1152]{1,0:T(8,128)(2,1)S(1)}, f16[96,1152]{1,0:T(8,128)(2,1)S(1)}, u32[]{:S(2)}, u32[]{:S(2)}) collective-permute-start(f16[96,1152]{1,0:T(8,128)(2,1)S(1)} %convert_element_type.48), channel_id=1, source_target_pairs={{0,1},{1,0},{2,3},{3,2},{4,5},{5,4},{6,7},{7,6},{8,9},{9,8},{10,11... | collective-permute-start | bytes 663560 | tf_op jit(solution)/shard_map/ppermute | solution.py:24
  90.5 3.8 %collective-permute-start.9 = (f16[96,1152]{1,0:T(8,128)(2,1)S(1)}, f16[96,1152]{1,0:T(8,128)(2,1)S(1)}, u32[]{:S(2)}, u32[]{:S(2)}) collective-permute-start(f16[96,1152]{1,0:T(8,128)(2,1)S(1)} %convert_element_type.46), channel_id=1, source_target_pairs={{0,1},{1,0},{2,3},{3,2},{4,5},{5,4},{6,7},{7,6},{8,9},{9,8},{10,11... | collective-permute-start | bytes 663560 | tf_op jit(solution)/shard_map/ppermute | solution.py:24
  94.3 5.9 %collective-permute-done.10 = f16[96,1152]{1,0:T(8,128)(2,1)S(1)} collective-permute-done((f16[96,1152]{1,0:T(8,128)(2,1)S(1)}, f16[96,1152]{1,0:T(8,128)(2,1)S(1)}, u32[]{:S(2)}, u32[]{:S(2)}) %collective-permute-start.10) | collective-permute-done | bytes 221216 | tf_op jit(solution)/shard_map/ppermute | solution.py:24
  100.5 2.6 %collective-permute-start.11 = (f16[96,1152]{1,0:T(8,128)(2,1)S(1)}, f16[96,1152]{1,0:T(8,128)(2,1)S(1)}, u32[]{:S(2)}, u32[]{:S(2)}) collective-permute-start(f16[96,1152]{1,0:T(8,128)(2,1)S(1)} %convert_element_type.50), channel_id=1, source_target_pairs={{0,2},{1,3},{2,0},{3,1},{4,6},{5,7},{6,4},{7,5},{8,10},{9,11},{10,... | collective-permute-start | bytes 663560 | tf_op jit(solution)/shard_map/ppermute | solution.py:24
  103.7 7.0 %collective-permute-start.15 = (f16[96,1152]{1,0:T(8,128)(2,1)S(1)}, f16[96,1152]{1,0:T(8,128)(2,1)S(1)}, u32[]{:S(2)}, u32[]{:S(2)}) collective-permute-start(f16[96,1152]{1,0:T(8,128)(2,1)S(1)} %convert_element_type.58), channel_id=1, source_target_pairs={{0,4},{1,5},{2,6},{3,7},{4,0},{5,1},{6,2},{7,3},{8,12},{9,13},{10,... | collective-permute-start | bytes 663560 | tf_op jit(solution)/shard_map/ppermute | solution.py:24
  111.0 11.1 %collective-permute-done.11 = f16[96,1152]{1,0:T(8,128)(2,1)S(1)} collective-permute-done((f16[96,1152]{1,0:T(8,128)(2,1)S(1)}, f16[96,1152]{1,0:T(8,128)(2,1)S(1)}, u32[]{:S(2)}, u32[]{:S(2)}) %collective-permute-start.11) | collective-permute-done | bytes 221216 | tf_op jit(solution)/shard_map/ppermute | solution.py:24
  122.4 7.8 %collective-permute-done.15 = f16[96,1152]{1,0:T(8,128)(2,1)S(1)} collective-permute-done((f16[96,1152]{1,0:T(8,128)(2,1)S(1)}, f16[96,1152]{1,0:T(8,128)(2,1)S(1)}, u32[]{:S(2)}, u32[]{:S(2)}) %collective-permute-start.15) | collective-permute-done | bytes 221216 | tf_op jit(solution)/shard_map/ppermute | solution.py:24
  (44 shorter events, 10.6 us)
Async XLA Ops:
  6.5 54.7 %all-gather.2.cloned.1.call-start = ((), (), s32[]{:S(2)}) async-start(), calls=%async_computation | async-start | bytes 3932160 | tf_op jit(solution)/shard_map/all_gather | solution.py:184
  7.3 27.4 %collective-permute-start.3 = (bf16[1136,128]{1,0:T(8,128)(2,1)}, bf16[1136,128]{1,0:T(8,128)(2,1)S(1)}, u32[]{:S(2)}, u32[]{:S(2)}) collective-permute-start(bf16[1136,128]{1,0:T(8,128)(2,1)} %bitcast.14), channel_id=1, source_target_pairs={{0,256},{1,257},{2,258},{3,259},{4,260},{5,261},{6,262},{7,263},{8... | collective-permute-start | bytes 872456 | tf_op jit(solution)/shard_map/ppermute | solution.py:24
  23.0 12.0 %collective-permute-start.2 = (bf16[1136,128]{1,0:T(8,128)(2,1)}, bf16[1136,128]{1,0:T(8,128)(2,1)S(1)}, u32[]{:S(2)}, u32[]{:S(2)}) collective-permute-start(bf16[1136,128]{1,0:T(8,128)(2,1)} %bitcast.15), channel_id=1, source_target_pairs={{0,64},{1,65},{2,66},{3,67},{4,68},{5,69},{6,70},{7,71},{8,72},{9,... | collective-permute-start | bytes 872456 | tf_op jit(solution)/shard_map/ppermute | solution.py:24
  26.4 13.5 %collective-permute-start.1 = (bf16[1136,128]{1,0:T(8,128)(2,1)}, bf16[1136,128]{1,0:T(8,128)(2,1)S(1)}, u32[]{:S(2)}, u32[]{:S(2)}) collective-permute-start(bf16[1136,128]{1,0:T(8,128)(2,1)} %bitcast.16), channel_id=1, source_target_pairs={{0,128},{1,129},{2,130},{3,131},{4,132},{5,133},{6,134},{7,135},{8... | collective-permute-start | bytes 872456 | tf_op jit(solution)/shard_map/ppermute | solution.py:24
  29.5 14.9 %collective-permute-start = (bf16[1136,128]{1,0:T(8,128)(2,1)}, bf16[1136,128]{1,0:T(8,128)(2,1)S(1)}, u32[]{:S(2)}, u32[]{:S(2)}) collective-permute-start(bf16[1136,128]{1,0:T(8,128)(2,1)} %bitcast.17), channel_id=1, source_target_pairs={{0,192},{1,193},{2,194},{3,195},{4,196},{5,197},{6,198},{7,199},{8... | collective-permute-start | bytes 872456 | tf_op jit(solution)/shard_map/ppermute | solution.py:24
  44.4 20.8 %collective-permute-start.7 = (bf16[1136,128]{1,0:T(8,128)(2,1)S(1)}, bf16[1136,128]{1,0:T(8,128)(2,1)S(1)}, u32[]{:S(2)}, u32[]{:S(2)}) collective-permute-start(bf16[1136,128]{1,0:T(8,128)(2,1)S(1)} %collective-permute-done.3), channel_id=1, source_target_pairs={{0,64},{1,65},{2,66},{3,67},{4,68},{5,69},{6,70},{7,71},{8,72},{9,... | collective-permute-start | bytes 872456 | tf_op jit(solution)/shard_map/ppermute | solution.py:24
  46.9 18.3 %collective-permute-start.6 = (bf16[1136,128]{1,0:T(8,128)(2,1)S(1)}, bf16[1136,128]{1,0:T(8,128)(2,1)S(1)}, u32[]{:S(2)}, u32[]{:S(2)}) collective-permute-start(bf16[1136,128]{1,0:T(8,128)(2,1)S(1)} %collective-permute-done.3), channel_id=1, source_target_pairs={{0,128},{1,129},{2,130},{3,131},{4,132},{5,133},{6,134},{7,135},{8... | collective-permute-start | bytes 872456 | tf_op jit(solution)/shard_map/ppermute | solution.py:24
  49.9 15.3 %collective-permute-start.5 = (bf16[1136,128]{1,0:T(8,128)(2,1)S(1)}, bf16[1136,128]{1,0:T(8,128)(2,1)S(1)}, u32[]{:S(2)}, u32[]{:S(2)}) collective-permute-start(bf16[1136,128]{1,0:T(8,128)(2,1)S(1)} %collective-permute-done.3), channel_id=1, source_target_pairs={{0,192},{1,193},{2,194},{3,195},{4,196},{5,197},{6,198},{7,199},{8... | collective-permute-start | bytes 872456 | tf_op jit(solution)/shard_map/ppermute | solution.py:24
  55.1 12.2 %collective-permute-start.4 = (bf16[4,1136,128]{2,1,0:T(8,128)(2,1)S(1)}, bf16[4,1136,128]{2,1,0:T(8,128)(2,1)S(1)}, u32[]{:S(2)}, u32[]{:S(2)}) collective-permute-start(bf16[4,1136,128]{2,1,0:T(8,128)(2,1)S(1)} %pad_maximum_fusion.s0), channel_id=1, source_target_pairs={{0,32},{1,33},{2,34},{3,35},{4,36},{5,37},{6,38},{7,39},{8,40},{9,... | collective-permute-start | bytes 3489800 | tf_op jit(solution)/shard_map/ppermute | solution.py:24
  61.2 1.9 %copy-start = (bf16[2048,768]{1,0:T(8,128)(2,1)S(1)}, bf16[2048,768]{1,0:T(8,128)(2,1)}, u32[]{:S(2)}) copy-start(bf16[2048,768]{1,0:T(8,128)(2,1)} %all-gather.2.cloned.1.call-done.all_ref) | copy-start | bytes 9437188
  65.3 5.5 %collective-permute-start.8 = (bf16[4,1136,128]{2,1,0:T(8,128)(2,1)S(1)}, bf16[4,1136,128]{2,1,0:T(8,128)(2,1)S(1)}, u32[]{:S(2)}, u32[]{:S(2)}) collective-permute-start(bf16[4,1136,128]{2,1,0:T(8,128)(2,1)S(1)} %pad_maximum_fusion.1.s1), channel_id=1, source_target_pairs={{0,32},{1,33},{2,34},{3,35},{4,36},{5,37},{6,38},{7,39},{8,40},{9,... | collective-permute-start | bytes 3489800 | tf_op jit(solution)/shard_map/ppermute | solution.py:24
  74.9 13.3 %collective-permute-start.13 = (f16[96,1152]{1,0:T(8,128)(2,1)S(1)}, f16[96,1152]{1,0:T(8,128)(2,1)S(1)}, u32[]{:S(2)}, u32[]{:S(2)}) collective-permute-start(f16[96,1152]{1,0:T(8,128)(2,1)S(1)} %convert_element_type.54), channel_id=1, source_target_pairs={{0,1},{1,0},{2,3},{3,2},{4,5},{5,4},{6,7},{7,6},{8,9},{9,8},{10,11... | collective-permute-start | bytes 663560 | tf_op jit(solution)/shard_map/ppermute | solution.py:24
  81.9 21.2 %collective-permute-start.12 = (f16[96,1152]{1,0:T(8,128)(2,1)S(1)}, f16[96,1152]{1,0:T(8,128)(2,1)S(1)}, u32[]{:S(2)}, u32[]{:S(2)}) collective-permute-start(f16[96,1152]{1,0:T(8,128)(2,1)S(1)} %convert_element_type.52), channel_id=1, source_target_pairs={{0,1},{1,0},{2,3},{3,2},{4,5},{5,4},{6,7},{7,6},{8,9},{9,8},{10,11... | collective-permute-start | bytes 663560 | tf_op jit(solution)/shard_map/ppermute | solution.py:24
  83.8 16.4 %collective-permute-start.10 = (f16[96,1152]{1,0:T(8,128)(2,1)S(1)}, f16[96,1152]{1,0:T(8,128)(2,1)S(1)}, u32[]{:S(2)}, u32[]{:S(2)}) collective-permute-start(f16[96,1152]{1,0:T(8,128)(2,1)S(1)} %convert_element_type.48), channel_id=1, source_target_pairs={{0,1},{1,0},{2,3},{3,2},{4,5},{5,4},{6,7},{7,6},{8,9},{9,8},{10,11... | collective-permute-start | bytes 663560 | tf_op jit(solution)/shard_map/ppermute | solution.py:24
  88.5 14.9 %collective-permute-start.14 = (f16[96,1152]{1,0:T(8,128)(2,1)S(1)}, f16[96,1152]{1,0:T(8,128)(2,1)S(1)}, u32[]{:S(2)}, u32[]{:S(2)}) collective-permute-start(f16[96,1152]{1,0:T(8,128)(2,1)S(1)} %convert_element_type.56), channel_id=1, source_target_pairs={{0,2},{1,3},{2,0},{3,1},{4,6},{5,7},{6,4},{7,5},{8,10},{9,11},{10,... | collective-permute-start | bytes 663560 | tf_op jit(solution)/shard_map/ppermute | solution.py:24
  90.5 20.3 %collective-permute-start.9 = (f16[96,1152]{1,0:T(8,128)(2,1)S(1)}, f16[96,1152]{1,0:T(8,128)(2,1)S(1)}, u32[]{:S(2)}, u32[]{:S(2)}) collective-permute-start(f16[96,1152]{1,0:T(8,128)(2,1)S(1)} %convert_element_type.46), channel_id=1, source_target_pairs={{0,1},{1,0},{2,3},{3,2},{4,5},{5,4},{6,7},{7,6},{8,9},{9,8},{10,11... | collective-permute-start | bytes 663560 | tf_op jit(solution)/shard_map/ppermute | solution.py:24
  100.5 21.6 %collective-permute-start.11 = (f16[96,1152]{1,0:T(8,128)(2,1)S(1)}, f16[96,1152]{1,0:T(8,128)(2,1)S(1)}, u32[]{:S(2)}, u32[]{:S(2)}) collective-permute-start(f16[96,1152]{1,0:T(8,128)(2,1)S(1)} %convert_element_type.50), channel_id=1, source_target_pairs={{0,2},{1,3},{2,0},{3,1},{4,6},{5,7},{6,4},{7,5},{8,10},{9,11},{10,... | collective-permute-start | bytes 663560 | tf_op jit(solution)/shard_map/ppermute | solution.py:24
  103.7 26.4 %collective-permute-start.15 = (f16[96,1152]{1,0:T(8,128)(2,1)S(1)}, f16[96,1152]{1,0:T(8,128)(2,1)S(1)}, u32[]{:S(2)}, u32[]{:S(2)}) collective-permute-start(f16[96,1152]{1,0:T(8,128)(2,1)S(1)} %convert_element_type.58), channel_id=1, source_target_pairs={{0,4},{1,5},{2,6},{3,7},{4,0},{5,1},{6,2},{7,3},{8,12},{9,13},{10,... | collective-permute-start | bytes 663560 | tf_op jit(solution)/shard_map/ppermute | solution.py:24
Sparse Core Ops, SparseCore 0:
  9.5 51.6 all-gather.1
